TPU v7x, 32 devices: a whole 2x2x4 slice. The times are simulated.
32 devices in a mesh: grp: 2 (over x), lon: 16 (over z, y, core).
Axes of the slice: x: 2, y: 2, z: 4, core: 2. Of those that a mesh axis runs over, the one named last changes fastest.
Arguments:
- adjoint_final: float32 [80, 16, 32, 128], P('grp', None, 'lon'), parts along dimension 0, may hold values from -6 to 6
- winds: float32 [4, 2, 16, 128, 32], P(None, None, None, 'lon'), may hold values from -0.4 to 0.4
- diffusivity: float32 [15, 32, 128], P(None, 'lon'), may hold values from 0.02 to 0.24
- observed_values: float32 [8192, 640], P(('grp', 'lon')), parts along dimension 0, may hold values from -6 to 6
- observed_band: int32 [8192, 1], P(('grp', 'lon')), parts along dimension 0, may hold values from 0 to 15; in each aligned block of 256 rows (0 to 255, 256 to 511, ...) at most 32 rows name the same one
- observed_cell: int32 [8192], P(('grp', 'lon')), parts along dimension 0, may hold values from 0 to 255
- observed_step: int32 [8192], P(('grp', 'lon')), parts along dimension 0, may hold values from 0 to 3
Outputs:
- adjoint_start: float32 [80, 16, 32, 128], P('grp', None, 'lon'), parts along dimension 0
- flux_sensitivity: float32 [80, 32, 128], P('grp', 'lon'), parts along dimension 0
There are 2 independent parts, one for each index of `grp`. A program takes and returns all parts, laid end to end along the dimension named above; an argument that names none is the same for every part. Nothing has to cross between parts.
Inputs may be any that keep to these rules, and one draw needn't show every extreme that they name: `observed_band`: among the observation rows of one device no band is named more than 32 times, a bound that some block reaches.
All inputs are finite; a program needn't handle non-finite values.
Results may differ from a plain program's by a relative error of at most 0.0003.
Values sent between devices are 32-bit elements; how exact they have to be, the bound alone decides.
A program may use at most 64 MiB of HBM per device.

v0:
```python
import functools

import jax
import jax.numpy as jnp
from jax import lax
from jax.experimental import pallas as pl
from jax.experimental.pallas import tpu as pltpu
from jax.sharding import PartitionSpec as P

SUB = 4
ROWS = 8


def chunk_sizes(tracers):
    units = tracers // ROWS
    first = (units + 1) // 2
    return [n * ROWS for n in (first, units - first) if n]


def shifted(block, axis, distance):
    devices = range(lax.axis_size(axis))
    route = [((i - distance) % len(devices), i) for i in devices]
    return lax.ppermute(block, axis, route)


def step_weights(winds):
    u, v = winds[:, 0], winds[:, 1]

    def upwind(c):
        m = jnp.abs(c)
        return [
            -(c + m) / 12.0,
            (8.0 * c + 4.0 * m) / 12.0,
            (4.0 * m - 8.0 * c) / 12.0,
            (c - m) / 12.0,
        ]

    lat = winds.shape[-1]
    place = jnp.arange(lat)
    inside = [
        jnp.where((place + k >= 0) & (place + k < lat), w, 0.0)
        for k, w in zip((-2, -1, 1, 2), upwind(v))
    ]
    centre = 1.0 - 0.5 * jnp.abs(u) - 0.5 * jnp.abs(v)
    return jnp.stack([centre] + inside + upwind(u), axis=1)


def step_kernel(halo, *refs):
    if halo:
        q_ref, west_ref, east_ref, flux_ref, f_ref, w_ref, r_ref = refs[:7]
        out_ref, oeast_ref, owest_ref, oflux_ref = refs[7:]
    else:
        q_ref, f_ref, w_ref, r_ref = refs[:4]
        out_ref, oeast_ref, owest_ref = refs[4:]
    levels, columns, tracers, lat = q_ref.shape

    @pl.loop(0, tracers // ROWS)
    def _(i):
        at = pl.ds(pl.multiple_of(i * ROWS, ROWS), ROWS)
        field = []
        for x in range(columns):
            q = [q_ref[l, x, at, :] for l in range(levels)]
            if halo:
                q = [q[l] + (west_ref[l, x, at, :] + east_ref[l, x, at, :]) for l in range(levels)]
                oflux_ref[x, at, :] = flux_ref[x, at, :] + q[0]
            q = [q[l] + f_ref[l, x, at, :] for l in range(levels)]
            for _ in range(SUB):
                flow = [r_ref[l, x : x + 1, :] * (q[l + 1] - q[l]) for l in range(levels - 1)]
                q = (
                    [q[0] + flow[0]]
                    + [q[l] + flow[l] - flow[l - 1] for l in range(1, levels - 1)]
                    + [q[levels - 1] - flow[levels - 2]]
                )
            for l in range(levels):
                out_ref[l, x, at, :] = q[l]
        for l in range(levels):
            q = [out_ref[l, x, at, :] for x in range(columns)]

            def w(k, x):
                return w_ref[k, l, x : x + 1, :]

            total = []
            for x in range(columns):
                t = w(0, x) * q[x]
                for k, offset in ((1, -2), (2, -1), (3, 1), (4, 2)):
                    t = t + pltpu.roll(w(k, x) * q[x], offset % lat, 1)
                total.append(t)
            last = columns - 1
            for k, offset in ((5, -2), (6, -1), (7, 1), (8, 2)):
                for x in range(columns):
                    if 0 <= x + offset < columns:
                        total[x + offset] = total[x + offset] + w(k, x) * q[x]
            for x in range(columns):
                out_ref[l, x, at, :] = total[x]
            oeast_ref[l, 0, at, :] = w(7, last) * q[last] + w(8, last - 1) * q[last - 1]
            oeast_ref[l, 1, at, :] = w(8, last) * q[last]
            owest_ref[l, 0, at, :] = w(5, 0) * q[0]
            owest_ref[l, 1, at, :] = w(6, 0) * q[0] + w(5, 1) * q[1]


def step(q, halos, flux, forcing, weights, rate):
    levels, columns, tracers, lat = q.shape
    whole = jax.ShapeDtypeStruct(q.shape, jnp.float32)
    edge = jax.ShapeDtypeStruct((levels, 2, tracers, lat), jnp.float32)
    outs = [whole, edge, edge]
    operands = [q]
    if halos:
        operands += [halos[0], halos[1], flux]
        outs.append(jax.ShapeDtypeStruct(flux.shape, jnp.float32))
    operands += [forcing, weights, rate]
    vmem = pl.BlockSpec(memory_space=pltpu.VMEM)
    size = q.size
    return pl.pallas_call(
        functools.partial(step_kernel, bool(halos)),
        out_shape=outs,
        in_specs=[vmem] * len(operands),
        out_specs=[vmem] * len(outs),
        compiler_params=pltpu.CompilerParams(vmem_limit_bytes=24 << 20),
        cost_estimate=pl.CostEstimate(flops=60 * size, bytes_accessed=32 * size, transcendentals=0),
    )(*operands)


def split(values):
    high = lax.reduce_precision(values, 8, 7)
    return high.astype(jnp.bfloat16), (values - high).astype(jnp.bfloat16)


def select(hot, values):
    high, low = split(values)
    dims = (((0,), (0,)), ((), ()))
    dot = functools.partial(
        lax.dot_general, dimension_numbers=dims, preferred_element_type=jnp.float32
    )
    return dot(hot, high) + dot(hot, low)


def body(
    adjoint_final, winds, diffusivity, observed_values, observed_band, observed_cell, observed_step
):
    tracers, levels, columns, lat = adjoint_final.shape
    steps = winds.shape[0]
    rows, payload = observed_values.shape
    bands = lax.axis_size("lon")
    capacity = max(2, (2 * rows + bands - 1) // bands)
    cells = columns * lat

    target = observed_band[:, 0]
    named = target[:, None] == jnp.arange(bands, dtype=jnp.int32)[None, :]
    counted = named.astype(jnp.float32)
    earlier = (jnp.arange(rows)[:, None] > jnp.arange(rows)[None, :]).astype(jnp.float32)
    before = jnp.dot(earlier, counted, preferred_element_type=jnp.float32)
    slot = jnp.sum(before * counted, axis=1).astype(jnp.int32)
    place = target * capacity + slot
    hot = place[:, None] == jnp.arange(bands * capacity, dtype=jnp.int32)[None, :]
    code = (observed_step * cells + observed_cell).astype(jnp.float32)
    send_code = jnp.sum(jnp.where(hot, code[:, None] + 1.0, 0.0), axis=0) - 1.0
    send_values = select(hot.astype(jnp.bfloat16), observed_values)

    lat_rows = winds.shape[3]
    parts = winds.reshape(steps * 2 * levels * lat_rows, bands, columns).transpose(1, 0, 2)
    small = jnp.concatenate(
        [parts.reshape(bands, -1), send_code.reshape(bands, capacity)], axis=1
    )
    small = lax.all_to_all(small, "lon", split_axis=0, concat_axis=0, tiled=True)
    recv_values = lax.all_to_all(send_values, "lon", split_axis=0, concat_axis=0, tiled=True)
    recv_code = small[:, -capacity:].reshape(-1).astype(jnp.int32)
    own = small[:, :-capacity].reshape(bands, steps, 2, levels, lat_rows, columns)
    own = own.transpose(1, 2, 3, 5, 0, 4).reshape(steps, 2, levels, columns, lat)
    weights = step_weights(own)

    by_level = recv_values.reshape(-1, tracers, levels).transpose(0, 2, 1).reshape(-1, payload)
    high, low = split(by_level)
    cell_hot = (
        recv_code[:, None] == jnp.arange(steps * cells, dtype=jnp.int32)[None, :]
    ).astype(jnp.bfloat16)
    cell_hot = cell_hot.reshape(-1, steps * columns, lat)

    def dot(part):
        return jnp.einsum("kp,ksy->spy", part, cell_hot, preferred_element_type=jnp.float32)

    forcing = (dot(high) + dot(low)).reshape(steps, columns, levels, tracers, lat)
    forcing = forcing.transpose(0, 2, 1, 3, 4)

    field = adjoint_final.transpose(1, 2, 0, 3)
    ends = []
    start = 0
    for size in chunk_sizes(tracers):
        ends.append((start, start + size))
        start += size
    states = [(field[:, :, a:b], None, None) for a, b in ends]
    for number, s in enumerate(reversed(range(steps))):
        moved = []
        for (a, b), (q, halos, flux) in zip(ends, states):
            if number == 1:
                flux = jnp.zeros((columns, b - a, lat), jnp.float32)
            out = step(q, halos, flux, forcing[s, :, :, a:b], weights[s], diffusivity)
            halos = (shifted(out[1], "lon", 1), shifted(out[2], "lon", -1))
            moved.append((out[0], halos, out[3] if number else None))
        states = moved
    fields, fluxes = [], []
    for q, halos, flux in states:
        q = q.at[:, 0:2].add(halos[0])
        q = q.at[:, columns - 2 : columns].add(halos[1])
        fields.append(q)
        fluxes.append(flux + q[0])
    field = jnp.concatenate(fields, axis=2).transpose(2, 0, 1, 3)
    return field, jnp.concatenate(fluxes, axis=1).transpose(1, 0, 2)


def solution(mesh):
    return jax.shard_map(
        body,
        mesh=mesh,
        in_specs=(
            P("grp", None, "lon", None),
            P(None, None, None, "lon", None),
            P(None, "lon", None),
            P(("grp", "lon"), None),
            P(("grp", "lon"), None),
            P(("grp", "lon")),
            P(("grp", "lon")),
        ),
        out_specs=(P("grp", None, "lon", None), P("grp", "lon", None)),
        check_vma=False,
    )
```

profile of v0, /device:TPU:12, one launch (start us, length us, event | category | flops | bytes accessed | tf_op | source)
XLA Modules:
  0.0 145.7 jit_solution(5120974326831458740)
XLA Ops:
  0.6 1.0 fusion.7
  1.6 0.7 multiply_add_fusion.1
  2.3 0.7 convert_add_fusion
  3.2 2.8 %copy.82 = f32[4,2,16,8,32]{3,2,1,0,4:T(8,128)S(1)} copy(f32[4,2,16,8,32]{4,3,2,1,0:T(8,128)} %param.24) | data formatting | bytes 262144 | tf_op args[1]
  6.0 1.1 reshape.218
  7.1 0.5 copy.83
  8.0 0.8 all_to_all.14
  8.7 6.2 %all-to-all-start = ((f32[16,1,2080]{2,1,0:T(1,128)}), f32[16,1,2080]{2,1,0:T(1,128)S(1)}, u32[]{:S(2)}, u32[]{:S(2)}) async-start(f32[16,1,2080]{2,1,0:T(1,128)} %all_to_all.14), calls=%async_computation | async-start | bytes 278528 | tf_op jit(solution)/shard_map/all_to_all | solution.py:164
  15.5 0.5 fusion.13
  16.0 1.6 %convolution_add_fusion = f32[512,640]{1,0:T(8,128)} fusion(f32[512,640]{1,0:T(8,128)S(1)} %fusion.13, f32[256,640]{1,0:T(8,128)S(1)} %copy-done.1, s32[256]{0:T(256)S(1)} %bitcast.90), kind=kOutput, calls=%fused_computation.8 | convolution fusion | flops 168722432 | bytes 3277824 | tf_op jit(solution)/shard_map/dot_general | solution.py:134
  17.7 2.3 %all-to-all-done = f32[16,1,2080]{2,1,0:T(1,128)S(1)} async-done(((f32[16,1,2080]{2,1,0:T(1,128)}), f32[16,1,2080]{2,1,0:T(1,128)S(1)}, u32[]{:S(2)}, u32[]{:S(2)}) %all-to-all-start) | async-done | bytes 133152 | tf_op jit(solution)/shard_map/all_to_all | solution.py:164
  19.9 6.7 %all-to-all-start.1 = ((f32[16,32,640]{2,1,0:T(8,128)}), f32[16,32,640]{2,1,0:T(8,128)S(1)}, u32[]{:S(2)}, u32[]{:S(2)}) async-start(f32[16,32,640]{2,1,0:T(8,128)} %bitcast.6), calls=%async_computation.1 | async-start | bytes 2621440 | tf_op jit(solution)/shard_map/all_to_all | solution.py:165
  26.7 1.3 copy.92
  28.0 2.4 %copy.93 = f32[4,2,16,2,16,8]{2,5,4,3,1,0:T(8,128)} copy(f32[4,2,16,2,16,8]{4,3,5,2,1,0:T(2,128)} %bitcast.80) | data formatting | bytes 262144 | tf_op jit(solution)/shard_map/transpose | solution.py:168
  30.4 2.1 %fusion.35 = (f32[4,1,16,2,128]{2,4,3,1,0:T(8,128)S(1)}, f32[4,1,16,2,128]{2,4,3,1,0:T(8,128)}) fusion(f32[4,2,16,2,128]{2,4,3,1,0:T(8,128)} %bitcast.79), kind=kLoop, calls=%fused_computation.86 | loop fusion | bytes 262144 | tf_op jit(solution)/shard_map/slice | solution.py:27
  32.5 1.2 copy.103
  34.7 22.4 %all-to-all-done.1 = f32[16,32,640]{2,1,0:T(8,128)S(1)} async-done(((f32[16,32,640]{2,1,0:T(8,128)}), f32[16,32,640]{2,1,0:T(8,128)S(1)}, u32[]{:S(2)}, u32[]{:S(2)}) %all-to-all-start.1) | async-done | bytes 1310752 | tf_op jit(solution)/shard_map/all_to_all | solution.py:165
  57.1 4.7 %copy.85 = f32[16,32,640]{1,0,2:T(8,128)} copy(f32[16,32,640]{2,1,0:T(8,128)S(1)} %all-to-all-done.1) | data formatting | bytes 2621440 | tf_op jit(solution)/shard_map/all_to_all | solution.py:165
  61.8 4.3 %reshape.220 = f32[512,40,16]{0,2,1:T(8,128)S(1)} reshape(f32[16,32,640]{1,0,2:T(8,128)} %copy.85) | data formatting | bytes 2621440 | tf_op jit(solution)/shard_map/reshape | solution.py:171
  67.2 1.0 fusion
  68.2 2.6 %add_bitcast_fusion = f32[8,640,128]{1,2,0:T(8,128)} fusion(f32[8,128,640]{2,1,0:T(8,128)S(1)} %fusion, bf16[512,640,1]{0,1,2:T(8,128)(2,1)S(1)} %bitcast.81, s32[8,128]{1,0:T(8,128)S(1)} %multiply_add_fusion, s32[512]{0:T(512)S(1)} %convert_element_type.52), kind=kOutput, calls=%fused_computation.5 | convolution fusion | flops 672268288 | bytes 5904384 | tf_op jit(solution)/shard_map/kp,ksy->spy/dot_general | solution.py:179
  70.8 3.3 %copy.90 = f32[8,640,128]{2,1,0:T(8,128)} copy(f32[8,640,128]{1,2,0:T(8,128)} %add_bitcast_fusion) | data formatting | bytes 5242880 | tf_op jit(solution)/shard_map/add | solution.py:181
  74.1 2.0 %copy.108 = f32[4,2,16,40,128]{4,3,1,2,0:T(8,128)S(1)} copy(f32[4,2,16,40,128]{4,3,2,1,0:T(8,128)} %bitcast.77) | data formatting | bytes 5242880 | tf_op jit(solution)/shard_map/reshape | solution.py:181
  76.2 0.6 copy-done
  76.8 0.7 shard_map.106
  77.8 1.4 collective-permute-start.1
  80.1 1.5 %collective-permute-start.9 = (f32[16,2,16,128]{3,2,1,0:T(8,128)S(1)}, f32[16,2,16,128]{3,2,1,0:T(8,128)S(1)}, u32[]{:S(2)}, u32[]{:S(2)}) collective-permute-start(f32[16,2,16,128]{3,2,1,0:T(8,128)S(1)} %get-tuple-element.128), channel_id=1, source_target_pairs={{1,0},{2,1},{3,2},{4,3},{5,4},{6,5},{7,6},{8,7},{9,8},{10,9},{11,1... | collective-permute-start | bytes 786440 | tf_op jit(solution)/shard_map/ppermute | solution.py:23
  81.7 10.1 %collective-permute-done.refs_1_ = f32[16,2,24,128]{3,2,1,0:T(8,128)S(1)} collective-permute-done((f32[16,2,24,128]{3,2,1,0:T(8,128)S(1)}, f32[16,2,24,128]{3,2,1,0:T(8,128)S(1)}, u32[]{:S(2)}, u32[]{:S(2)}) %collective-permute-start) | collective-permute-done | bytes 393248 | tf_op jit(solution)/shard_map/ppermute | solution.py:23
  91.8 2.3 %collective-permute-done.1.refs_2_ = f32[16,2,24,128]{3,2,1,0:T(8,128)S(1)} collective-permute-done((f32[16,2,24,128]{3,2,1,0:T(8,128)S(1)}, f32[16,2,24,128]{3,2,1,0:T(8,128)S(1)}, u32[]{:S(2)}, u32[]{:S(2)}) %collective-permute-start.1) | collective-permute-done | bytes 393248 | tf_op jit(solution)/shard_map/ppermute | solution.py:23
  94.1 0.7 shard_map.107
  94.9 2.0 %collective-permute-start.3 = (f32[16,2,24,128]{3,2,1,0:T(8,128)S(1)}, f32[16,2,24,128]{3,2,1,0:T(8,128)S(1)}, u32[]{:S(2)}, u32[]{:S(2)}) collective-permute-start(f32[16,2,24,128]{3,2,1,0:T(8,128)S(1)} %get-tuple-element.117), channel_id=1, source_target_pairs={{1,0},{2,1},{3,2},{4,3},{5,4},{6,5},{7,6},{8,7},{9,8},{10,9},{11,1... | collective-permute-start | bytes 1179656 | tf_op jit(solution)/shard_map/ppermute | solution.py:23
  96.9 0.5 shard_map.111
  97.5 2.0 %collective-permute-start.11 = (f32[16,2,16,128]{3,2,1,0:T(8,128)S(1)}, f32[16,2,16,128]{3,2,1,0:T(8,128)S(1)}, u32[]{:S(2)}, u32[]{:S(2)}) collective-permute-start(f32[16,2,16,128]{3,2,1,0:T(8,128)S(1)} %get-tuple-element.131), channel_id=1, source_target_pairs={{1,0},{2,1},{3,2},{4,3},{5,4},{6,5},{7,6},{8,7},{9,8},{10,9},{11,1... | collective-permute-start | bytes 786440 | tf_op jit(solution)/shard_map/ppermute | solution.py:23
  99.4 12.7 %collective-permute-done.10.refs_1_ = f32[16,2,16,128]{3,2,1,0:T(8,128)S(1)} collective-permute-done((f32[16,2,16,128]{3,2,1,0:T(8,128)S(1)}, f32[16,2,16,128]{3,2,1,0:T(8,128)S(1)}, u32[]{:S(2)}, u32[]{:S(2)}) %collective-permute-start.10) | collective-permute-done | bytes 262176 | tf_op jit(solution)/shard_map/ppermute | solution.py:23
  112.1 0.5 shard_map.112
  112.6 1.7 %collective-permute-start.13 = (f32[16,2,16,128]{3,2,1,0:T(8,128)S(1)}, f32[16,2,16,128]{3,2,1,0:T(8,128)S(1)}, u32[]{:S(2)}, u32[]{:S(2)}) collective-permute-start(f32[16,2,16,128]{3,2,1,0:T(8,128)S(1)} %get-tuple-element.135), channel_id=1, source_target_pairs={{1,0},{2,1},{3,2},{4,3},{5,4},{6,5},{7,6},{8,7},{9,8},{10,9},{11,1... | collective-permute-start | bytes 786440 | tf_op jit(solution)/shard_map/ppermute | solution.py:23
  114.4 0.7 shard_map.108
  115.2 1.7 %collective-permute-start.5 = (f32[16,2,24,128]{3,2,1,0:T(8,128)S(1)}, f32[16,2,24,128]{3,2,1,0:T(8,128)S(1)}, u32[]{:S(2)}, u32[]{:S(2)}) collective-permute-start(f32[16,2,24,128]{3,2,1,0:T(8,128)S(1)} %get-tuple-element.121), channel_id=1, source_target_pairs={{1,0},{2,1},{3,2},{4,3},{5,4},{6,5},{7,6},{8,7},{9,8},{10,9},{11,1... | collective-permute-start | bytes 1179656 | tf_op jit(solution)/shard_map/ppermute | solution.py:23
  116.9 8.5 %collective-permute-done.12.refs_1_ = f32[16,2,16,128]{3,2,1,0:T(8,128)S(1)} collective-permute-done((f32[16,2,16,128]{3,2,1,0:T(8,128)S(1)}, f32[16,2,16,128]{3,2,1,0:T(8,128)S(1)}, u32[]{:S(2)}, u32[]{:S(2)}) %collective-permute-start.12) | collective-permute-done | bytes 262176 | tf_op jit(solution)/shard_map/ppermute | solution.py:23
  125.4 0.5 shard_map.113
  126.0 1.8 %collective-permute-start.15 = (f32[16,2,16,128]{3,2,1,0:T(8,128)S(1)}, f32[16,2,16,128]{3,2,1,0:T(8,128)S(1)}, u32[]{:S(2)}, u32[]{:S(2)}) collective-permute-start(f32[16,2,16,128]{3,2,1,0:T(8,128)S(1)} %get-tuple-element.139), channel_id=1, source_target_pairs={{1,0},{2,1},{3,2},{4,3},{5,4},{6,5},{7,6},{8,7},{9,8},{10,9},{11,1... | collective-permute-start | bytes 786440 | tf_op jit(solution)/shard_map/ppermute | solution.py:23
  127.8 1.9 %collective-permute-done.4.refs_1_ = f32[16,2,24,128]{3,2,1,0:T(8,128)S(1)} collective-permute-done((f32[16,2,24,128]{3,2,1,0:T(8,128)S(1)}, f32[16,2,24,128]{3,2,1,0:T(8,128)S(1)}, u32[]{:S(2)}, u32[]{:S(2)}) %collective-permute-start.4) | collective-permute-done | bytes 393248 | tf_op jit(solution)/shard_map/ppermute | solution.py:23
  129.7 0.7 shard_map.109
  130.4 1.8 %collective-permute-start.7 = (f32[16,2,24,128]{3,2,1,0:T(8,128)S(1)}, f32[16,2,24,128]{3,2,1,0:T(8,128)S(1)}, u32[]{:S(2)}, u32[]{:S(2)}) collective-permute-start(f32[16,2,24,128]{3,2,1,0:T(8,128)S(1)} %get-tuple-element.125), channel_id=1, source_target_pairs={{1,0},{2,1},{3,2},{4,3},{5,4},{6,5},{7,6},{8,7},{9,8},{10,9},{11,1... | collective-permute-start | bytes 1179656 | tf_op jit(solution)/shard_map/ppermute | solution.py:23
  132.2 7.2 %collective-permute-done.14 = f32[16,2,16,128]{3,2,1,0:T(8,128)S(1)} collective-permute-done((f32[16,2,16,128]{3,2,1,0:T(8,128)S(1)}, f32[16,2,16,128]{3,2,1,0:T(8,128)S(1)}, u32[]{:S(2)}, u32[]{:S(2)}) %collective-permute-start.14) | collective-permute-done | bytes 262176 | tf_op jit(solution)/shard_map/ppermute | solution.py:23
  139.6 4.1 %collective-permute-done.6 = f32[16,2,24,128]{3,2,1,0:T(8,128)S(1)} collective-permute-done((f32[16,2,24,128]{3,2,1,0:T(8,128)S(1)}, f32[16,2,24,128]{3,2,1,0:T(8,128)S(1)}, u32[]{:S(2)}, u32[]{:S(2)}) %collective-permute-start.6) | collective-permute-done | bytes 393248 | tf_op jit(solution)/shard_map/ppermute | solution.py:23
  143.9 0.6 copy.97
  144.5 1.2 copy.96
  (65 shorter events, 4.9 us)
Async XLA Ops:
  7.1 7.9 %copy-start.2 = (f32[40,16,2,128]{3,2,1,0:T(2,128)S(1)}, f32[40,16,2,128]{3,2,1,0:T(2,128)}, u32[]{:S(2)}) copy-start(f32[40,16,2,128]{3,2,1,0:T(2,128)} %param.23) | copy-start | bytes 1966084
  7.6 7.9 %copy-start.1 = (f32[256,640]{1,0:T(8,128)S(1)}, f32[256,640]{1,0:T(8,128)}, u32[]{:S(2)}) copy-start(f32[256,640]{1,0:T(8,128)} %param.26) | copy-start | bytes 1966084
  8.7 11.2 %all-to-all-start = ((f32[16,1,2080]{2,1,0:T(1,128)}), f32[16,1,2080]{2,1,0:T(1,128)S(1)}, u32[]{:S(2)}, u32[]{:S(2)}) async-start(f32[16,1,2080]{2,1,0:T(1,128)} %all_to_all.14), calls=%async_computation | async-start | bytes 278528 | tf_op jit(solution)/shard_map/all_to_all | solution.py:164
  19.9 37.2 %all-to-all-start.1 = ((f32[16,32,640]{2,1,0:T(8,128)}), f32[16,32,640]{2,1,0:T(8,128)S(1)}, u32[]{:S(2)}, u32[]{:S(2)}) async-start(f32[16,32,640]{2,1,0:T(8,128)} %bitcast.6), calls=%async_computation.1 | async-start | bytes 2621440 | tf_op jit(solution)/shard_map/all_to_all | solution.py:165
  76.1 0.7 copy-start
  77.5 14.3 %collective-permute-start = (f32[16,2,24,128]{3,2,1,0:T(8,128)S(1)}, f32[16,2,24,128]{3,2,1,0:T(8,128)S(1)}, u32[]{:S(2)}, u32[]{:S(2)}) collective-permute-start(f32[16,2,24,128]{3,2,1,0:T(8,128)S(1)} %get-tuple-element.113), channel_id=1, source_target_pairs={{15,0},{0,1},{1,2},{2,3},{3,4},{4,5},{5,6},{6,7},{7,8},{8,9},{9,10... | collective-permute-start | bytes 1179656 | tf_op jit(solution)/shard_map/ppermute | solution.py:23
  77.8 16.3 %collective-permute-start.1 = (f32[16,2,24,128]{3,2,1,0:T(8,128)S(1)}, f32[16,2,24,128]{3,2,1,0:T(8,128)S(1)}, u32[]{:S(2)}, u32[]{:S(2)}) collective-permute-start(f32[16,2,24,128]{3,2,1,0:T(8,128)S(1)} %get-tuple-element.114), channel_id=1, source_target_pairs={{1,0},{2,1},{3,2},{4,3},{5,4},{6,5},{7,6},{8,7},{9,8},{10,9},{11,1... | collective-permute-start | bytes 1179656 | tf_op jit(solution)/shard_map/ppermute | solution.py:23
  79.9 17.0 %collective-permute-start.8 = (f32[16,2,16,128]{3,2,1,0:T(8,128)S(1)}, f32[16,2,16,128]{3,2,1,0:T(8,128)S(1)}, u32[]{:S(2)}, u32[]{:S(2)}) collective-permute-start(f32[16,2,16,128]{3,2,1,0:T(8,128)S(1)} %get-tuple-element.127), channel_id=1, source_target_pairs={{15,0},{0,1},{1,2},{2,3},{3,4},{4,5},{5,6},{6,7},{7,8},{8,9},{9,10... | collective-permute-start | bytes 786440 | tf_op jit(solution)/shard_map/ppermute | solution.py:23
  80.1 16.8 %collective-permute-start.9 = (f32[16,2,16,128]{3,2,1,0:T(8,128)S(1)}, f32[16,2,16,128]{3,2,1,0:T(8,128)S(1)}, u32[]{:S(2)}, u32[]{:S(2)}) collective-permute-start(f32[16,2,16,128]{3,2,1,0:T(8,128)S(1)} %get-tuple-element.128), channel_id=1, source_target_pairs={{1,0},{2,1},{3,2},{4,3},{5,4},{6,5},{7,6},{8,7},{9,8},{10,9},{11,1... | collective-permute-start | bytes 786440 | tf_op jit(solution)/shard_map/ppermute | solution.py:23
  94.8 19.5 %collective-permute-start.2 = (f32[16,2,24,128]{3,2,1,0:T(8,128)S(1)}, f32[16,2,24,128]{3,2,1,0:T(8,128)S(1)}, u32[]{:S(2)}, u32[]{:S(2)}) collective-permute-start(f32[16,2,24,128]{3,2,1,0:T(8,128)S(1)} %get-tuple-element.116), channel_id=1, source_target_pairs={{15,0},{0,1},{1,2},{2,3},{3,4},{4,5},{5,6},{6,7},{7,8},{8,9},{9,10... | collective-permute-start | bytes 1179656 | tf_op jit(solution)/shard_map/ppermute | solution.py:23
  94.9 19.5 %collective-permute-start.3 = (f32[16,2,24,128]{3,2,1,0:T(8,128)S(1)}, f32[16,2,24,128]{3,2,1,0:T(8,128)S(1)}, u32[]{:S(2)}, u32[]{:S(2)}) collective-permute-start(f32[16,2,24,128]{3,2,1,0:T(8,128)S(1)} %get-tuple-element.117), channel_id=1, source_target_pairs={{1,0},{2,1},{3,2},{4,3},{5,4},{6,5},{7,6},{8,7},{9,8},{10,9},{11,1... | collective-permute-start | bytes 1179656 | tf_op jit(solution)/shard_map/ppermute | solution.py:23
  97.4 14.7 %collective-permute-start.10 = (f32[16,2,16,128]{3,2,1,0:T(8,128)S(1)}, f32[16,2,16,128]{3,2,1,0:T(8,128)S(1)}, u32[]{:S(2)}, u32[]{:S(2)}) collective-permute-start(f32[16,2,16,128]{3,2,1,0:T(8,128)S(1)} %get-tuple-element.130), channel_id=1, source_target_pairs={{15,0},{0,1},{1,2},{2,3},{3,4},{4,5},{5,6},{6,7},{7,8},{8,9},{9,10... | collective-permute-start | bytes 786440 | tf_op jit(solution)/shard_map/ppermute | solution.py:23
  97.5 14.6 %collective-permute-start.11 = (f32[16,2,16,128]{3,2,1,0:T(8,128)S(1)}, f32[16,2,16,128]{3,2,1,0:T(8,128)S(1)}, u32[]{:S(2)}, u32[]{:S(2)}) collective-permute-start(f32[16,2,16,128]{3,2,1,0:T(8,128)S(1)} %get-tuple-element.131), channel_id=1, source_target_pairs={{1,0},{2,1},{3,2},{4,3},{5,4},{6,5},{7,6},{8,7},{9,8},{10,9},{11,1... | collective-permute-start | bytes 786440 | tf_op jit(solution)/shard_map/ppermute | solution.py:23
  112.6 12.9 %collective-permute-start.12 = (f32[16,2,16,128]{3,2,1,0:T(8,128)S(1)}, f32[16,2,16,128]{3,2,1,0:T(8,128)S(1)}, u32[]{:S(2)}, u32[]{:S(2)}) collective-permute-start(f32[16,2,16,128]{3,2,1,0:T(8,128)S(1)} %get-tuple-element.134), channel_id=1, source_target_pairs={{15,0},{0,1},{1,2},{2,3},{3,4},{4,5},{5,6},{6,7},{7,8},{8,9},{9,10... | collective-permute-start | bytes 786440 | tf_op jit(solution)/shard_map/ppermute | solution.py:23
  112.6 12.8 %collective-permute-start.13 = (f32[16,2,16,128]{3,2,1,0:T(8,128)S(1)}, f32[16,2,16,128]{3,2,1,0:T(8,128)S(1)}, u32[]{:S(2)}, u32[]{:S(2)}) collective-permute-start(f32[16,2,16,128]{3,2,1,0:T(8,128)S(1)} %get-tuple-element.135), channel_id=1, source_target_pairs={{1,0},{2,1},{3,2},{4,3},{5,4},{6,5},{7,6},{8,7},{9,8},{10,9},{11,1... | collective-permute-start | bytes 786440 | tf_op jit(solution)/shard_map/ppermute | solution.py:23
  115.1 14.6 %collective-permute-start.4 = (f32[16,2,24,128]{3,2,1,0:T(8,128)S(1)}, f32[16,2,24,128]{3,2,1,0:T(8,128)S(1)}, u32[]{:S(2)}, u32[]{:S(2)}) collective-permute-start(f32[16,2,24,128]{3,2,1,0:T(8,128)S(1)} %get-tuple-element.120), channel_id=1, source_target_pairs={{15,0},{0,1},{1,2},{2,3},{3,4},{4,5},{5,6},{6,7},{7,8},{8,9},{9,10... | collective-permute-start | bytes 1179656 | tf_op jit(solution)/shard_map/ppermute | solution.py:23
  115.2 14.5 %collective-permute-start.5 = (f32[16,2,24,128]{3,2,1,0:T(8,128)S(1)}, f32[16,2,24,128]{3,2,1,0:T(8,128)S(1)}, u32[]{:S(2)}, u32[]{:S(2)}) collective-permute-start(f32[16,2,24,128]{3,2,1,0:T(8,128)S(1)} %get-tuple-element.121), channel_id=1, source_target_pairs={{1,0},{2,1},{3,2},{4,3},{5,4},{6,5},{7,6},{8,7},{9,8},{10,9},{11,1... | collective-permute-start | bytes 1179656 | tf_op jit(solution)/shard_map/ppermute | solution.py:23
  125.9 13.5 %collective-permute-start.14 = (f32[16,2,16,128]{3,2,1,0:T(8,128)S(1)}, f32[16,2,16,128]{3,2,1,0:T(8,128)S(1)}, u32[]{:S(2)}, u32[]{:S(2)}) collective-permute-start(f32[16,2,16,128]{3,2,1,0:T(8,128)S(1)} %get-tuple-element.138), channel_id=1, source_target_pairs={{15,0},{0,1},{1,2},{2,3},{3,4},{4,5},{5,6},{6,7},{7,8},{8,9},{9,10... | collective-permute-start | bytes 786440 | tf_op jit(solution)/shard_map/ppermute | solution.py:23
  126.0 13.5 %collective-permute-start.15 = (f32[16,2,16,128]{3,2,1,0:T(8,128)S(1)}, f32[16,2,16,128]{3,2,1,0:T(8,128)S(1)}, u32[]{:S(2)}, u32[]{:S(2)}) collective-permute-start(f32[16,2,16,128]{3,2,1,0:T(8,128)S(1)} %get-tuple-element.139), channel_id=1, source_target_pairs={{1,0},{2,1},{3,2},{4,3},{5,4},{6,5},{7,6},{8,7},{9,8},{10,9},{11,1... | collective-permute-start | bytes 786440 | tf_op jit(solution)/shard_map/ppermute | solution.py:23
  130.4 13.3 %collective-permute-start.6 = (f32[16,2,24,128]{3,2,1,0:T(8,128)S(1)}, f32[16,2,24,128]{3,2,1,0:T(8,128)S(1)}, u32[]{:S(2)}, u32[]{:S(2)}) collective-permute-start(f32[16,2,24,128]{3,2,1,0:T(8,128)S(1)} %get-tuple-element.124), channel_id=1, source_target_pairs={{15,0},{0,1},{1,2},{2,3},{3,4},{4,5},{5,6},{6,7},{7,8},{8,9},{9,10... | collective-permute-start | bytes 1179656 | tf_op jit(solution)/shard_map/ppermute | solution.py:23
  130.4 13.3 %collective-permute-start.7 = (f32[16,2,24,128]{3,2,1,0:T(8,128)S(1)}, f32[16,2,24,128]{3,2,1,0:T(8,128)S(1)}, u32[]{:S(2)}, u32[]{:S(2)}) collective-permute-start(f32[16,2,24,128]{3,2,1,0:T(8,128)S(1)} %get-tuple-element.125), channel_id=1, source_target_pairs={{1,0},{2,1},{3,2},{4,3},{5,4},{6,5},{7,6},{8,7},{9,8},{10,9},{11,1... | collective-permute-start | bytes 1179656 | tf_op jit(solution)/shard_map/ppermute | solution.py:23
where the time goes:
time: 146 us
  waiting for transfers between devices  71.6 us (49%)
  local copies, waits for them, and re-layouts  31 us (21%)
  starting transfers between devices  27.9 us (19%)
  matrix products  6.73 us (5%)
  Pallas kernels  4.75 us (3%)
  other arithmetic  2.71 us (2%)
    ppermute x16, waiting for transfers between devices, shifted(): return lax.ppermute(block, axis, route)  46.9 us
    all_to_all x1, waiting for transfers between devices, body(): lax.all_to_all(send_values, 'lon', split_axis=0, concat_axis=0, tiled=True)  22.4 us
    ppermute x16, starting transfers between devices, shifted(): return lax.ppermute(block, axis, route)  14.9 us
    unnamed x13, local copies, waits for them, and re-layouts  6.99 us
    all_to_all x1, starting transfers between devices, body(): lax.all_to_all(send_values, 'lon', split_axis=0, concat_axis=0, tiled=True)  6.73 us
    all_to_all x1, starting transfers between devices, body(): lax.all_to_all(small, 'lon', split_axis=0, concat_axis=0, tiled=True)  6.24 us
    pallas_call x8, Pallas kernels, step(): pl.pallas_call(functools.partial(step_kernel, bool(halos)), out_shape=out...  4.75 us
    all_to_all x1, local copies, waits for them, and re-layouts, body(): lax.all_to_all(send_values, 'lon', split_axis=0, concat_axis=0, tiled=True)  4.74 us
  transfers between devices with their start and end apart: 18, of which 10 were waited for; matrix products, arithmetic and copies ran while one was open for 7% of the time, Pallas kernels for 3%

commit v1 on v0

--- a/solution.py
+++ b/solution.py
@@ -45,7 +45,7 @@
     return jnp.stack([centre] + inside + upwind(u), axis=1)
 
 
-def step_kernel(halo, *refs):
+def step_kernel(halo, start, *refs):
     if halo:
         q_ref, west_ref, east_ref, flux_ref, f_ref, w_ref, r_ref = refs[:7]
         out_ref, oeast_ref, owest_ref, oflux_ref = refs[7:]
@@ -57,13 +57,13 @@
     @pl.loop(0, tracers // ROWS)
     def _(i):
         at = pl.ds(pl.multiple_of(i * ROWS, ROWS), ROWS)
-        field = []
+        own = pl.ds(pl.multiple_of(start + i * ROWS, ROWS), ROWS)
         for x in range(columns):
             q = [q_ref[l, x, at, :] for l in range(levels)]
             if halo:
                 q = [q[l] + (west_ref[l, x, at, :] + east_ref[l, x, at, :]) for l in range(levels)]
                 oflux_ref[x, at, :] = flux_ref[x, at, :] + q[0]
-            q = [q[l] + f_ref[l, x, at, :] for l in range(levels)]
+            q = [q[l] + f_ref[x, l, own, :] for l in range(levels)]
             for _ in range(SUB):
                 flow = [r_ref[l, x : x + 1, :] * (q[l + 1] - q[l]) for l in range(levels - 1)]
                 q = (
@@ -98,7 +98,7 @@
             owest_ref[l, 1, at, :] = w(6, 0) * q[0] + w(5, 1) * q[1]
 
 
-def step(q, halos, flux, forcing, weights, rate):
+def step(q, halos, flux, forcing, weights, rate, start):
     levels, columns, tracers, lat = q.shape
     whole = jax.ShapeDtypeStruct(q.shape, jnp.float32)
     edge = jax.ShapeDtypeStruct((levels, 2, tracers, lat), jnp.float32)
@@ -111,7 +111,7 @@
     vmem = pl.BlockSpec(memory_space=pltpu.VMEM)
     size = q.size
     return pl.pallas_call(
-        functools.partial(step_kernel, bool(halos)),
+        functools.partial(step_kernel, bool(halos), start),
         out_shape=outs,
         in_specs=[vmem] * len(operands),
         out_specs=[vmem] * len(outs),
@@ -120,18 +120,35 @@
     )(*operands)
 
 
+def forcing_kernel(first, code_ref, high_ref, low_ref, out_ref):
+    columns, _, lat = out_ref.shape
+    for x in range(columns):
+        cell = first + x * lat + lax.broadcasted_iota(jnp.int32, (code_ref.shape[0], lat), 1)
+        hot = jnp.where(code_ref[...] == cell, 1.0, 0.0).astype(jnp.bfloat16)
+        total = jnp.dot(high_ref[...], hot, preferred_element_type=jnp.float32)
+        out_ref[x] = total + jnp.dot(low_ref[...], hot, preferred_element_type=jnp.float32)
+
+
+def step_forcing(code, high, low, first, columns, lat):
+    payload, slots = high.shape
+    vmem = pl.BlockSpec(memory_space=pltpu.VMEM)
+    return pl.pallas_call(
+        functools.partial(forcing_kernel, first),
+        out_shape=jax.ShapeDtypeStruct((columns, payload, lat), jnp.float32),
+        in_specs=[vmem] * 3,
+        out_specs=vmem,
+        compiler_params=pltpu.CompilerParams(vmem_limit_bytes=24 << 20),
+        cost_estimate=pl.CostEstimate(
+            flops=4 * payload * slots * columns * lat,
+            bytes_accessed=4 * payload * (slots + columns * lat),
+            transcendentals=0,
+        ),
+    )(code, high, low)
+
+
 def split(values):
     high = lax.reduce_precision(values, 8, 7)
     return high.astype(jnp.bfloat16), (values - high).astype(jnp.bfloat16)
-
-
-def select(hot, values):
-    high, low = split(values)
-    dims = (((0,), (0,)), ((), ()))
-    dot = functools.partial(
-        lax.dot_general, dimension_numbers=dims, preferred_element_type=jnp.float32
-    )
-    return dot(hot, high) + dot(hot, low)
 
 
 def body(
@@ -154,7 +171,17 @@
     hot = place[:, None] == jnp.arange(bands * capacity, dtype=jnp.int32)[None, :]
     code = (observed_step * cells + observed_cell).astype(jnp.float32)
     send_code = jnp.sum(jnp.where(hot, code[:, None] + 1.0, 0.0), axis=0) - 1.0
-    send_values = select(hot.astype(jnp.bfloat16), observed_values)
+    column = jnp.arange(payload, dtype=jnp.int32)
+    source = (column % tracers) * levels + column // tracers
+    swap = (column[:, None] == source[None, :]).astype(jnp.bfloat16)
+    high, low = split(observed_values)
+    dims = (((0,), (0,)), ((), ()))
+    send_values = 0.0
+    for part in (high, low):
+        part = jnp.dot(part, swap, preferred_element_type=jnp.float32).astype(jnp.bfloat16)
+        send_values = send_values + lax.dot_general(
+            hot.astype(jnp.bfloat16), part, dims, preferred_element_type=jnp.float32
+        )
 
     lat_rows = winds.shape[3]
     parts = winds.reshape(steps * 2 * levels * lat_rows, bands, columns).transpose(1, 0, 2)
@@ -168,18 +195,8 @@
     own = own.transpose(1, 2, 3, 5, 0, 4).reshape(steps, 2, levels, columns, lat)
     weights = step_weights(own)
 
-    by_level = recv_values.reshape(-1, tracers, levels).transpose(0, 2, 1).reshape(-1, payload)
-    high, low = split(by_level)
-    cell_hot = (
-        recv_code[:, None] == jnp.arange(steps * cells, dtype=jnp.int32)[None, :]
-    ).astype(jnp.bfloat16)
-    cell_hot = cell_hot.reshape(-1, steps * columns, lat)
-
-    def dot(part):
-        return jnp.einsum("kp,ksy->spy", part, cell_hot, preferred_element_type=jnp.float32)
-
-    forcing = (dot(high) + dot(low)).reshape(steps, columns, levels, tracers, lat)
-    forcing = forcing.transpose(0, 2, 1, 3, 4)
+    high, low = split(recv_values.T)
+    code = recv_code[:, None]
 
     field = adjoint_final.transpose(1, 2, 0, 3)
     ends = []
@@ -190,10 +207,12 @@
     states = [(field[:, :, a:b], None, None) for a, b in ends]
     for number, s in enumerate(reversed(range(steps))):
         moved = []
+        forcing = step_forcing(code, high, low, s * cells, columns, lat)
+        forcing = forcing.reshape(columns, levels, tracers, lat)
         for (a, b), (q, halos, flux) in zip(ends, states):
             if number == 1:
                 flux = jnp.zeros((columns, b - a, lat), jnp.float32)
-            out = step(q, halos, flux, forcing[s, :, :, a:b], weights[s], diffusivity)
+            out = step(q, halos, flux, forcing, weights[s], diffusivity, a)
             halos = (shifted(out[1], "lon", 1), shifted(out[2], "lon", -1))
             moved.append((out[0], halos, out[3] if number else None))
         states = moved

time: 146 us -> 131 us (0.90)
  local copies, waits for them, and re-layouts: 31 us -> 17.8 us
  waiting for transfers between devices: 71.6 us -> 66.4 us
  Pallas kernels: 4.75 us -> 8.61 us
  matrix products: 6.73 us -> 4.01 us
    reshape x2 -> x0, local copies, waits for them, and re-layouts: 6.3 us -> none  [the longest x1 4.33 us: body(): recv_values.reshape(-1, tracers, levels).transpose(0, 2, 1)]
    ppermute x16, waiting for transfers between devices: 46.9 us -> 43 us  [shifted(): return lax.ppermute(block, axis, route)]
    pallas_call x8 -> x12, Pallas kernels: 4.75 us -> 8.61 us  [the longest x8 4.8 us: step(): pl.pallas_call(functools.partial(step_kernel, bool(halos), start), out_sh...]
    add x1 -> x0, local copies, waits for them, and re-layouts: 3.26 us -> none  [body(): dot(high) + dot(low)]
    all_to_all x1, local copies, waits for them, and re-layouts: 4.74 us -> 1.48 us  [body(): lax.all_to_all(send_values, 'lon', split_axis=0, concat_axis=0, tiled=True)]
    dot_general x4 -> x2, matrix products: 5.78 us -> 3.06 us  [body(): lax.dot_general(hot.astype(jnp.bfloat16), part, dims, preferred_element_t...]
    all_to_all x1, waiting for transfers between devices: 2.27 us -> 0.54 us  [body(): lax.all_to_all(small, 'lon', split_axis=0, concat_axis=0, tiled=True)]
    unnamed x13 -> x15, local copies, waits for them, and re-layouts: 6.99 us -> 8.28 us
  transfers between devices with their start and end apart: 18 -> 18, of which waited for: 10 -> 9; matrix products, arithmetic and copies ran while one was open for 7% -> 9% of each run, Pallas kernels for 3% -> 5%
where the time goes in v1:
time: 131 us; the launch traced here: 130 us
  waiting for transfers between devices  66.4 us (51%)
  starting transfers between devices  28.1 us (21%)
  local copies, waits for them, and re-layouts  17.8 us (14%)
  Pallas kernels  8.61 us (7%)
  matrix products  4.01 us (3%)
  other arithmetic  3.99 us (3%)
    ppermute x16, waiting for transfers between devices, shifted(): return lax.ppermute(block, axis, route)  43 us
    all_to_all x1, waiting for transfers between devices, body(): lax.all_to_all(send_values, 'lon', split_axis=0, concat_axis=0, tiled=True)  22.9 us
    ppermute x16, starting transfers between devices, shifted(): return lax.ppermute(block, axis, route)  15.1 us
    unnamed x15, local copies, waits for them, and re-layouts  8.28 us
    all_to_all x1, starting transfers between devices, body(): lax.all_to_all(send_values, 'lon', split_axis=0, concat_axis=0, tiled=True)  6.73 us
    all_to_all x1, starting transfers between devices, body(): lax.all_to_all(small, 'lon', split_axis=0, concat_axis=0, tiled=True)  6.24 us
    pallas_call x8, Pallas kernels, step(): pl.pallas_call(functools.partial(step_kernel, bool(halos), start), out_sh...  4.8 us
    pallas_call x4, Pallas kernels, step_forcing(): pl.pallas_call(functools.partial(forcing_kernel, first), out_shape=jax.Sh...  3.81 us
  transfers between devices with their start and end apart: 18, of which 9 were waited for; matrix products, arithmetic and copies ran while one was open for 9% of the time, Pallas kernels for 5%

profile of v1, /device:TPU:12, one launch (start us, length us, event | category | flops | bytes accessed | tf_op | source)
XLA Modules:
  0.0 130.0 jit_solution(12878244483238472876)
XLA Ops:
  0.6 1.0 fusion.5
  1.6 0.7 multiply_add_fusion
  2.3 0.7 convert_add_fusion
  3.2 2.8 %copy.76 = f32[4,2,16,8,32]{3,2,1,0,4:T(8,128)S(1)} copy(f32[4,2,16,8,32]{4,3,2,1,0:T(8,128)} %param.24) | data formatting | bytes 262144 | tf_op args[1]
  6.0 1.1 reshape.225
  7.1 0.5 copy.77
  8.0 0.7 all_to_all.16
  8.7 6.2 %all-to-all-start = ((f32[16,1,2080]{2,1,0:T(1,128)}), f32[16,1,2080]{2,1,0:T(1,128)S(1)}, u32[]{:S(2)}, u32[]{:S(2)}) async-start(f32[16,1,2080]{2,1,0:T(1,128)} %all_to_all.16), calls=%async_computation | async-start | bytes 278528 | tf_op jit(solution)/shard_map/all_to_all | solution.py:191
  15.4 0.8 copy-done.1
  16.3 0.8 fusion.4
  17.2 2.2 %convolution_add_fusion = f32[512,640]{1,0:T(8,128)} fusion(f32[512,640]{1,0:T(8,128)S(1)} %fusion.4, s32[640]{0:T(1024)S(1)} %fusion.43, f32[256,640]{1,0:T(8,128)S(1)} %copy-done.3, s32[256]{0:T(256)S(1)} %bitcast.67), kind=kOutput, calls=%fused_computation.5 | convolution fusion | flops 379387904 | bytes 3280384 | tf_op jit(solution)/shard_map/dot_general | solution.py:182
  19.4 0.5 all-to-all-done
  19.9 6.7 %all-to-all-start.1 = ((f32[16,32,640]{2,1,0:T(8,128)}), f32[16,32,640]{2,1,0:T(8,128)S(1)}, u32[]{:S(2)}, u32[]{:S(2)}) async-start(f32[16,32,640]{2,1,0:T(8,128)} %bitcast.6), calls=%async_computation.1 | async-start | bytes 2621440 | tf_op jit(solution)/shard_map/all_to_all | solution.py:192
  26.9 1.3 %copy.81 = f32[16,2048]{0,1:T(8,128)} copy(f32[16,2048]{1,0:T(8,128)S(1)} %slice.150) | data formatting | bytes 262144 | tf_op jit(solution)/shard_map/slice | solution.py:194
  28.3 1.6 %copy.82 = f32[4,2,16,2,16,8]{2,5,4,3,1,0:T(8,128)S(1)} copy(f32[4,2,16,2,16,8]{4,3,5,2,1,0:T(2,128)} %bitcast.59) | data formatting | bytes 262144 | tf_op jit(solution)/shard_map/transpose | solution.py:195
  29.9 1.1 fusion.46
  31.0 1.2 copy.92
  32.2 1.2 copy.91
  34.2 22.9 %all-to-all-done.1 = f32[16,32,640]{2,1,0:T(8,128)S(1)} async-done(((f32[16,32,640]{2,1,0:T(8,128)}), f32[16,32,640]{2,1,0:T(8,128)S(1)}, u32[]{:S(2)}, u32[]{:S(2)}) %all-to-all-start.1) | async-done | bytes 1310752 | tf_op jit(solution)/shard_map/all_to_all | solution.py:192
  57.1 1.5 %copy.79 = f32[512,640]{0,1:T(8,128)} copy(f32[512,640]{1,0:T(8,128)S(1)} %bitcast.56) | data formatting | bytes 2621440 | tf_op jit(solution)/shard_map/all_to_all | solution.py:192
  58.6 1.5 %fusion.2 = (bf16[640,512]{1,0:T(8,128)(2,1)S(1)}, bf16[640,512]{1,0:T(8,128)(2,1)S(1)}) fusion(f32[512,640]{0,1:T(8,128)} %copy.79), kind=kLoop, calls=%fused_computation.6 | loop fusion | flops 1310720 | bytes 2621440 | tf_op jit(solution)/shard_map/convert_element_type | solution.py:151
  60.1 1.0 shard_map.106
  61.1 0.7 shard_map.107
  62.1 1.4 %collective-permute-start.1 = (f32[16,2,24,128]{3,2,1,0:T(8,128)S(1)}, f32[16,2,24,128]{3,2,1,0:T(8,128)S(1)}, u32[]{:S(2)}, u32[]{:S(2)}) collective-permute-start(f32[16,2,24,128]{3,2,1,0:T(8,128)S(1)} %get-tuple-element.114), channel_id=1, source_target_pairs={{1,0},{2,1},{3,2},{4,3},{5,4},{6,5},{7,6},{8,7},{9,8},{10,9},{11,1... | collective-permute-start | bytes 1179656 | tf_op jit(solution)/shard_map/ppermute | solution.py:23
  63.6 1.0 slice.157.refs_0_
  65.3 1.5 %collective-permute-start.9 = (f32[16,2,16,128]{3,2,1,0:T(8,128)S(1)}, f32[16,2,16,128]{3,2,1,0:T(8,128)S(1)}, u32[]{:S(2)}, u32[]{:S(2)}) collective-permute-start(f32[16,2,16,128]{3,2,1,0:T(8,128)S(1)} %get-tuple-element.128), channel_id=1, source_target_pairs={{1,0},{2,1},{3,2},{4,3},{5,4},{6,5},{7,6},{8,7},{9,8},{10,9},{11,1... | collective-permute-start | bytes 786440 | tf_op jit(solution)/shard_map/ppermute | solution.py:23
  66.8 1.0 shard_map.108
  67.8 8.3 %collective-permute-done.refs_1_ = f32[16,2,24,128]{3,2,1,0:T(8,128)S(1)} collective-permute-done((f32[16,2,24,128]{3,2,1,0:T(8,128)S(1)}, f32[16,2,24,128]{3,2,1,0:T(8,128)S(1)}, u32[]{:S(2)}, u32[]{:S(2)}) %collective-permute-start) | collective-permute-done | bytes 393248 | tf_op jit(solution)/shard_map/ppermute | solution.py:23
  76.0 2.3 %collective-permute-done.1.refs_2_ = f32[16,2,24,128]{3,2,1,0:T(8,128)S(1)} collective-permute-done((f32[16,2,24,128]{3,2,1,0:T(8,128)S(1)}, f32[16,2,24,128]{3,2,1,0:T(8,128)S(1)}, u32[]{:S(2)}, u32[]{:S(2)}) %collective-permute-start.1) | collective-permute-done | bytes 393248 | tf_op jit(solution)/shard_map/ppermute | solution.py:23
  78.4 0.7 shard_map.109
  79.2 2.0 %collective-permute-start.3 = (f32[16,2,24,128]{3,2,1,0:T(8,128)S(1)}, f32[16,2,24,128]{3,2,1,0:T(8,128)S(1)}, u32[]{:S(2)}, u32[]{:S(2)}) collective-permute-start(f32[16,2,24,128]{3,2,1,0:T(8,128)S(1)} %get-tuple-element.117), channel_id=1, source_target_pairs={{1,0},{2,1},{3,2},{4,3},{5,4},{6,5},{7,6},{8,7},{9,8},{10,9},{11,1... | collective-permute-start | bytes 1179656 | tf_op jit(solution)/shard_map/ppermute | solution.py:23
  81.7 2.1 %collective-permute-start.11 = (f32[16,2,16,128]{3,2,1,0:T(8,128)S(1)}, f32[16,2,16,128]{3,2,1,0:T(8,128)S(1)}, u32[]{:S(2)}, u32[]{:S(2)}) collective-permute-start(f32[16,2,16,128]{3,2,1,0:T(8,128)S(1)} %get-tuple-element.131), channel_id=1, source_target_pairs={{1,0},{2,1},{3,2},{4,3},{5,4},{6,5},{7,6},{8,7},{9,8},{10,9},{11,1... | collective-permute-start | bytes 786440 | tf_op jit(solution)/shard_map/ppermute | solution.py:23
  83.9 1.0 shard_map.110
  84.8 11.5 %collective-permute-done.10.refs_1_ = f32[16,2,16,128]{3,2,1,0:T(8,128)S(1)} collective-permute-done((f32[16,2,16,128]{3,2,1,0:T(8,128)S(1)}, f32[16,2,16,128]{3,2,1,0:T(8,128)S(1)}, u32[]{:S(2)}, u32[]{:S(2)}) %collective-permute-start.10) | collective-permute-done | bytes 262176 | tf_op jit(solution)/shard_map/ppermute | solution.py:23
  96.4 0.5 shard_map.116
  96.9 1.7 %collective-permute-start.13 = (f32[16,2,16,128]{3,2,1,0:T(8,128)S(1)}, f32[16,2,16,128]{3,2,1,0:T(8,128)S(1)}, u32[]{:S(2)}, u32[]{:S(2)}) collective-permute-start(f32[16,2,16,128]{3,2,1,0:T(8,128)S(1)} %get-tuple-element.135), channel_id=1, source_target_pairs={{1,0},{2,1},{3,2},{4,3},{5,4},{6,5},{7,6},{8,7},{9,8},{10,9},{11,1... | collective-permute-start | bytes 786440 | tf_op jit(solution)/shard_map/ppermute | solution.py:23
  98.7 0.7 shard_map.111
  99.5 1.7 %collective-permute-start.5 = (f32[16,2,24,128]{3,2,1,0:T(8,128)S(1)}, f32[16,2,24,128]{3,2,1,0:T(8,128)S(1)}, u32[]{:S(2)}, u32[]{:S(2)}) collective-permute-start(f32[16,2,24,128]{3,2,1,0:T(8,128)S(1)} %get-tuple-element.121), channel_id=1, source_target_pairs={{1,0},{2,1},{3,2},{4,3},{5,4},{6,5},{7,6},{8,7},{9,8},{10,9},{11,1... | collective-permute-start | bytes 1179656 | tf_op jit(solution)/shard_map/ppermute | solution.py:23
  101.2 1.0 shard_map.112
  102.2 7.6 %collective-permute-done.12.refs_1_ = f32[16,2,16,128]{3,2,1,0:T(8,128)S(1)} collective-permute-done((f32[16,2,16,128]{3,2,1,0:T(8,128)S(1)}, f32[16,2,16,128]{3,2,1,0:T(8,128)S(1)}, u32[]{:S(2)}, u32[]{:S(2)}) %collective-permute-start.12) | collective-permute-done | bytes 262176 | tf_op jit(solution)/shard_map/ppermute | solution.py:23
  110.3 1.8 %collective-permute-start.15 = (f32[16,2,16,128]{3,2,1,0:T(8,128)S(1)}, f32[16,2,16,128]{3,2,1,0:T(8,128)S(1)}, u32[]{:S(2)}, u32[]{:S(2)}) collective-permute-start(f32[16,2,16,128]{3,2,1,0:T(8,128)S(1)} %get-tuple-element.139), channel_id=1, source_target_pairs={{1,0},{2,1},{3,2},{4,3},{5,4},{6,5},{7,6},{8,7},{9,8},{10,9},{11,1... | collective-permute-start | bytes 786440 | tf_op jit(solution)/shard_map/ppermute | solution.py:23
  112.1 1.8 %collective-permute-done.4.refs_1_ = f32[16,2,24,128]{3,2,1,0:T(8,128)S(1)} collective-permute-done((f32[16,2,24,128]{3,2,1,0:T(8,128)S(1)}, f32[16,2,24,128]{3,2,1,0:T(8,128)S(1)}, u32[]{:S(2)}, u32[]{:S(2)}) %collective-permute-start.4) | collective-permute-done | bytes 393248 | tf_op jit(solution)/shard_map/ppermute | solution.py:23
  113.9 0.7 shard_map.113
  114.7 1.8 %collective-permute-start.7 = (f32[16,2,24,128]{3,2,1,0:T(8,128)S(1)}, f32[16,2,24,128]{3,2,1,0:T(8,128)S(1)}, u32[]{:S(2)}, u32[]{:S(2)}) collective-permute-start(f32[16,2,24,128]{3,2,1,0:T(8,128)S(1)} %get-tuple-element.125), channel_id=1, source_target_pairs={{1,0},{2,1},{3,2},{4,3},{5,4},{6,5},{7,6},{8,7},{9,8},{10,9},{11,1... | collective-permute-start | bytes 1179656 | tf_op jit(solution)/shard_map/ppermute | solution.py:23
  116.5 7.2 %collective-permute-done.14 = f32[16,2,16,128]{3,2,1,0:T(8,128)S(1)} collective-permute-done((f32[16,2,16,128]{3,2,1,0:T(8,128)S(1)}, f32[16,2,16,128]{3,2,1,0:T(8,128)S(1)}, u32[]{:S(2)}, u32[]{:S(2)}) %collective-permute-start.14) | collective-permute-done | bytes 262176 | tf_op jit(solution)/shard_map/ppermute | solution.py:23
  123.9 4.1 %collective-permute-done.6 = f32[16,2,24,128]{3,2,1,0:T(8,128)S(1)} collective-permute-done((f32[16,2,24,128]{3,2,1,0:T(8,128)S(1)}, f32[16,2,24,128]{3,2,1,0:T(8,128)S(1)}, u32[]{:S(2)}, u32[]{:S(2)}) %collective-permute-start.6) | collective-permute-done | bytes 393248 | tf_op jit(solution)/shard_map/ppermute | solution.py:23
  128.2 1.2 copy.88
  129.3 0.6 copy.89
  (62 shorter events, 4.7 us)
Async XLA Ops:
  7.1 7.9 %copy-start.2 = (f32[40,16,2,128]{3,2,1,0:T(2,128)S(1)}, f32[40,16,2,128]{3,2,1,0:T(2,128)}, u32[]{:S(2)}) copy-start(f32[40,16,2,128]{3,2,1,0:T(2,128)} %param.23) | copy-start | bytes 1966084
  8.0 8.3 %copy-start.3 = (f32[256,640]{1,0:T(8,128)S(1)}, f32[256,640]{1,0:T(8,128)}, u32[]{:S(2)}) copy-start(f32[256,640]{1,0:T(8,128)} %param.26) | copy-start | bytes 1966084
  8.7 11.2 %all-to-all-start = ((f32[16,1,2080]{2,1,0:T(1,128)}), f32[16,1,2080]{2,1,0:T(1,128)S(1)}, u32[]{:S(2)}, u32[]{:S(2)}) async-start(f32[16,1,2080]{2,1,0:T(1,128)} %all_to_all.16), calls=%async_computation | async-start | bytes 278528 | tf_op jit(solution)/shard_map/all_to_all | solution.py:191
  15.4 0.8 copy-start.1
  19.9 37.2 %all-to-all-start.1 = ((f32[16,32,640]{2,1,0:T(8,128)}), f32[16,32,640]{2,1,0:T(8,128)S(1)}, u32[]{:S(2)}, u32[]{:S(2)}) async-start(f32[16,32,640]{2,1,0:T(8,128)} %bitcast.6), calls=%async_computation.1 | async-start | bytes 2621440 | tf_op jit(solution)/shard_map/all_to_all | solution.py:192
  60.1 1.0 copy-start
  61.8 14.3 %collective-permute-start = (f32[16,2,24,128]{3,2,1,0:T(8,128)S(1)}, f32[16,2,24,128]{3,2,1,0:T(8,128)S(1)}, u32[]{:S(2)}, u32[]{:S(2)}) collective-permute-start(f32[16,2,24,128]{3,2,1,0:T(8,128)S(1)} %get-tuple-element.113), channel_id=1, source_target_pairs={{15,0},{0,1},{1,2},{2,3},{3,4},{4,5},{5,6},{6,7},{7,8},{8,9},{9,10... | collective-permute-start | bytes 1179656 | tf_op jit(solution)/shard_map/ppermute | solution.py:23
  62.1 16.3 %collective-permute-start.1 = (f32[16,2,24,128]{3,2,1,0:T(8,128)S(1)}, f32[16,2,24,128]{3,2,1,0:T(8,128)S(1)}, u32[]{:S(2)}, u32[]{:S(2)}) collective-permute-start(f32[16,2,24,128]{3,2,1,0:T(8,128)S(1)} %get-tuple-element.114), channel_id=1, source_target_pairs={{1,0},{2,1},{3,2},{4,3},{5,4},{6,5},{7,6},{8,7},{9,8},{10,9},{11,1... | collective-permute-start | bytes 1179656 | tf_op jit(solution)/shard_map/ppermute | solution.py:23
  65.0 16.1 %collective-permute-start.8 = (f32[16,2,16,128]{3,2,1,0:T(8,128)S(1)}, f32[16,2,16,128]{3,2,1,0:T(8,128)S(1)}, u32[]{:S(2)}, u32[]{:S(2)}) collective-permute-start(f32[16,2,16,128]{3,2,1,0:T(8,128)S(1)} %get-tuple-element.127), channel_id=1, source_target_pairs={{15,0},{0,1},{1,2},{2,3},{3,4},{4,5},{5,6},{6,7},{7,8},{8,9},{9,10... | collective-permute-start | bytes 786440 | tf_op jit(solution)/shard_map/ppermute | solution.py:23
  65.3 15.9 %collective-permute-start.9 = (f32[16,2,16,128]{3,2,1,0:T(8,128)S(1)}, f32[16,2,16,128]{3,2,1,0:T(8,128)S(1)}, u32[]{:S(2)}, u32[]{:S(2)}) collective-permute-start(f32[16,2,16,128]{3,2,1,0:T(8,128)S(1)} %get-tuple-element.128), channel_id=1, source_target_pairs={{1,0},{2,1},{3,2},{4,3},{5,4},{6,5},{7,6},{8,7},{9,8},{10,9},{11,1... | collective-permute-start | bytes 786440 | tf_op jit(solution)/shard_map/ppermute | solution.py:23
  79.1 19.6 %collective-permute-start.2 = (f32[16,2,24,128]{3,2,1,0:T(8,128)S(1)}, f32[16,2,24,128]{3,2,1,0:T(8,128)S(1)}, u32[]{:S(2)}, u32[]{:S(2)}) collective-permute-start(f32[16,2,24,128]{3,2,1,0:T(8,128)S(1)} %get-tuple-element.116), channel_id=1, source_target_pairs={{15,0},{0,1},{1,2},{2,3},{3,4},{4,5},{5,6},{6,7},{7,8},{8,9},{9,10... | collective-permute-start | bytes 1179656 | tf_op jit(solution)/shard_map/ppermute | solution.py:23
  79.2 19.5 %collective-permute-start.3 = (f32[16,2,24,128]{3,2,1,0:T(8,128)S(1)}, f32[16,2,24,128]{3,2,1,0:T(8,128)S(1)}, u32[]{:S(2)}, u32[]{:S(2)}) collective-permute-start(f32[16,2,24,128]{3,2,1,0:T(8,128)S(1)} %get-tuple-element.117), channel_id=1, source_target_pairs={{1,0},{2,1},{3,2},{4,3},{5,4},{6,5},{7,6},{8,7},{9,8},{10,9},{11,1... | collective-permute-start | bytes 1179656 | tf_op jit(solution)/shard_map/ppermute | solution.py:23
  81.7 14.7 %collective-permute-start.10 = (f32[16,2,16,128]{3,2,1,0:T(8,128)S(1)}, f32[16,2,16,128]{3,2,1,0:T(8,128)S(1)}, u32[]{:S(2)}, u32[]{:S(2)}) collective-permute-start(f32[16,2,16,128]{3,2,1,0:T(8,128)S(1)} %get-tuple-element.130), channel_id=1, source_target_pairs={{15,0},{0,1},{1,2},{2,3},{3,4},{4,5},{5,6},{6,7},{7,8},{8,9},{9,10... | collective-permute-start | bytes 786440 | tf_op jit(solution)/shard_map/ppermute | solution.py:23
  81.7 14.6 %collective-permute-start.11 = (f32[16,2,16,128]{3,2,1,0:T(8,128)S(1)}, f32[16,2,16,128]{3,2,1,0:T(8,128)S(1)}, u32[]{:S(2)}, u32[]{:S(2)}) collective-permute-start(f32[16,2,16,128]{3,2,1,0:T(8,128)S(1)} %get-tuple-element.131), channel_id=1, source_target_pairs={{1,0},{2,1},{3,2},{4,3},{5,4},{6,5},{7,6},{8,7},{9,8},{10,9},{11,1... | collective-permute-start | bytes 786440 | tf_op jit(solution)/shard_map/ppermute | solution.py:23
  96.9 12.9 %collective-permute-start.12 = (f32[16,2,16,128]{3,2,1,0:T(8,128)S(1)}, f32[16,2,16,128]{3,2,1,0:T(8,128)S(1)}, u32[]{:S(2)}, u32[]{:S(2)}) collective-permute-start(f32[16,2,16,128]{3,2,1,0:T(8,128)S(1)} %get-tuple-element.134), channel_id=1, source_target_pairs={{15,0},{0,1},{1,2},{2,3},{3,4},{4,5},{5,6},{6,7},{7,8},{8,9},{9,10... | collective-permute-start | bytes 786440 | tf_op jit(solution)/shard_map/ppermute | solution.py:23
  96.9 12.8 %collective-permute-start.13 = (f32[16,2,16,128]{3,2,1,0:T(8,128)S(1)}, f32[16,2,16,128]{3,2,1,0:T(8,128)S(1)}, u32[]{:S(2)}, u32[]{:S(2)}) collective-permute-start(f32[16,2,16,128]{3,2,1,0:T(8,128)S(1)} %get-tuple-element.135), channel_id=1, source_target_pairs={{1,0},{2,1},{3,2},{4,3},{5,4},{6,5},{7,6},{8,7},{9,8},{10,9},{11,1... | collective-permute-start | bytes 786440 | tf_op jit(solution)/shard_map/ppermute | solution.py:23
  99.4 14.5 %collective-permute-start.4 = (f32[16,2,24,128]{3,2,1,0:T(8,128)S(1)}, f32[16,2,24,128]{3,2,1,0:T(8,128)S(1)}, u32[]{:S(2)}, u32[]{:S(2)}) collective-permute-start(f32[16,2,24,128]{3,2,1,0:T(8,128)S(1)} %get-tuple-element.120), channel_id=1, source_target_pairs={{15,0},{0,1},{1,2},{2,3},{3,4},{4,5},{5,6},{6,7},{7,8},{8,9},{9,10... | collective-permute-start | bytes 1179656 | tf_op jit(solution)/shard_map/ppermute | solution.py:23
  99.5 14.5 %collective-permute-start.5 = (f32[16,2,24,128]{3,2,1,0:T(8,128)S(1)}, f32[16,2,24,128]{3,2,1,0:T(8,128)S(1)}, u32[]{:S(2)}, u32[]{:S(2)}) collective-permute-start(f32[16,2,24,128]{3,2,1,0:T(8,128)S(1)} %get-tuple-element.121), channel_id=1, source_target_pairs={{1,0},{2,1},{3,2},{4,3},{5,4},{6,5},{7,6},{8,7},{9,8},{10,9},{11,1... | collective-permute-start | bytes 1179656 | tf_op jit(solution)/shard_map/ppermute | solution.py:23
  110.2 13.5 %collective-permute-start.14 = (f32[16,2,16,128]{3,2,1,0:T(8,128)S(1)}, f32[16,2,16,128]{3,2,1,0:T(8,128)S(1)}, u32[]{:S(2)}, u32[]{:S(2)}) collective-permute-start(f32[16,2,16,128]{3,2,1,0:T(8,128)S(1)} %get-tuple-element.138), channel_id=1, source_target_pairs={{15,0},{0,1},{1,2},{2,3},{3,4},{4,5},{5,6},{6,7},{7,8},{8,9},{9,10... | collective-permute-start | bytes 786440 | tf_op jit(solution)/shard_map/ppermute | solution.py:23
  110.3 13.5 %collective-permute-start.15 = (f32[16,2,16,128]{3,2,1,0:T(8,128)S(1)}, f32[16,2,16,128]{3,2,1,0:T(8,128)S(1)}, u32[]{:S(2)}, u32[]{:S(2)}) collective-permute-start(f32[16,2,16,128]{3,2,1,0:T(8,128)S(1)} %get-tuple-element.139), channel_id=1, source_target_pairs={{1,0},{2,1},{3,2},{4,3},{5,4},{6,5},{7,6},{8,7},{9,8},{10,9},{11,1... | collective-permute-start | bytes 786440 | tf_op jit(solution)/shard_map/ppermute | solution.py:23
  114.7 13.3 %collective-permute-start.6 = (f32[16,2,24,128]{3,2,1,0:T(8,128)S(1)}, f32[16,2,24,128]{3,2,1,0:T(8,128)S(1)}, u32[]{:S(2)}, u32[]{:S(2)}) collective-permute-start(f32[16,2,24,128]{3,2,1,0:T(8,128)S(1)} %get-tuple-element.124), channel_id=1, source_target_pairs={{15,0},{0,1},{1,2},{2,3},{3,4},{4,5},{5,6},{6,7},{7,8},{8,9},{9,10... | collective-permute-start | bytes 1179656 | tf_op jit(solution)/shard_map/ppermute | solution.py:23
  114.7 13.2 %collective-permute-start.7 = (f32[16,2,24,128]{3,2,1,0:T(8,128)S(1)}, f32[16,2,24,128]{3,2,1,0:T(8,128)S(1)}, u32[]{:S(2)}, u32[]{:S(2)}) collective-permute-start(f32[16,2,24,128]{3,2,1,0:T(8,128)S(1)} %get-tuple-element.125), channel_id=1, source_target_pairs={{1,0},{2,1},{3,2},{4,3},{5,4},{6,5},{7,6},{8,7},{9,8},{10,9},{11,1... | collective-permute-start | bytes 1179656 | tf_op jit(solution)/shard_map/ppermute | solution.py:23

commit v2 on v1

--- a/solution.py
+++ b/solution.py
@@ -188,8 +188,16 @@
     small = jnp.concatenate(
         [parts.reshape(bands, -1), send_code.reshape(bands, capacity)], axis=1
     )
-    small = lax.all_to_all(small, "lon", split_axis=0, concat_axis=0, tiled=True)
-    recv_values = lax.all_to_all(send_values, "lon", split_axis=0, concat_axis=0, tiled=True)
+    length = small.shape[1]
+    extra = -(-length // payload)
+    small = jnp.pad(small, ((0, 0), (0, extra * payload - length)))
+    sent = jnp.concatenate(
+        [send_values.reshape(bands, capacity, payload), small.reshape(bands, extra, payload)],
+        axis=1,
+    )
+    received = lax.all_to_all(sent, "lon", split_axis=0, concat_axis=0, tiled=True)
+    recv_values = received[:, :capacity].reshape(-1, payload)
+    small = received[:, capacity:].reshape(bands, extra * payload)[:, :length]
     recv_code = small[:, -capacity:].reshape(-1).astype(jnp.int32)
     own = small[:, :-capacity].reshape(bands, steps, 2, levels, lat_rows, columns)
     own = own.transpose(1, 2, 3, 5, 0, 4).reshape(steps, 2, levels, columns, lat)

time: 131 us -> 136 us (1.038)
  waiting for transfers between devices: 66.4 us -> 78.8 us
  starting transfers between devices: 28.1 us -> 21.5 us
    all_to_all x2 -> x1, waiting for transfers between devices: 23.5 us -> 36.2 us  [body(): lax.all_to_all(sent, 'lon', split_axis=0, concat_axis=0, tiled=True)]
    all_to_all x2 -> x1, starting transfers between devices: 13 us -> 6.37 us  [body(): lax.all_to_all(sent, 'lon', split_axis=0, concat_axis=0, tiled=True)]
    slice x0 -> x2, local copies, waits for them, and re-layouts: none -> 2.41 us  [the longest x1 1.41 us: body(): recv_values = received[:, :capacity].reshape(-1, payload)]
    all_to_all x2 -> x0, local copies, waits for them, and re-layouts: 2.22 us -> none  [the longest x1 1.48 us: body(): lax.all_to_all(send_values, 'lon', split_axis=0, concat_axis=0, tiled=True)]
  transfers between devices with their start and end apart: 18 -> 17, of which waited for: 9 -> 9; matrix products, arithmetic and copies ran while one was open for 9% -> 1% of each run, Pallas kernels for 5% -> 5%
where the time goes in v2:
time: 136 us; the launch traced here: 135 us
  waiting for transfers between devices  78.8 us (58%)
  starting transfers between devices  21.5 us (16%)
  local copies, waits for them, and re-layouts  17.3 us (13%)
  Pallas kernels  8.61 us (6%)
  matrix products  4.02 us (3%)
  other arithmetic  3.91 us (3%)
    ppermute x16, waiting for transfers between devices, shifted(): return lax.ppermute(block, axis, route)  42.5 us
    all_to_all x1, waiting for transfers between devices, body(): lax.all_to_all(sent, 'lon', split_axis=0, concat_axis=0, tiled=True)  36.2 us
    ppermute x16, starting transfers between devices, shifted(): return lax.ppermute(block, axis, route)  15.1 us
    unnamed x15, local copies, waits for them, and re-layouts  7.24 us
    all_to_all x1, starting transfers between devices, body(): lax.all_to_all(sent, 'lon', split_axis=0, concat_axis=0, tiled=True)  6.37 us
    pallas_call x8, Pallas kernels, step(): pl.pallas_call(functools.partial(step_kernel, bool(halos), start), out_sh...  4.8 us
    pallas_call x4, Pallas kernels, step_forcing(): pl.pallas_call(functools.partial(forcing_kernel, first), out_shape=jax.Sh...  3.81 us
    dot_general x2, matrix products, body(): lax.dot_general(hot.astype(jnp.bfloat16), part, dims, preferred_element_t...  3.07 us
  transfers between devices with their start and end apart: 17, of which 9 were waited for; matrix products, arithmetic and copies ran while one was open for 1% of the time, Pallas kernels for 5%

profile of v2, /device:TPU:12, one launch (start us, length us, event | category | flops | bytes accessed | tf_op | source)
XLA Modules:
  0.0 135.1 jit_solution(16914460118620117102)
XLA Ops:
  0.7 1.0 fusion.5
  1.6 0.7 multiply_add_fusion
  2.3 0.7 convert_add_fusion
  3.2 1.9 %fusion.4 = f32[512,640]{1,0:T(8,128)S(1)} fusion(s32[640]{0:T(1024)S(1)} %fusion.43, f32[256,640]{1,0:T(8,128)} %param.26, s32[256]{0:T(256)S(1)} %bitcast.67), kind=kOutput, calls=%fused_computation.10 | convolution fusion | flops 378683392 | bytes 1969664 | tf_op jit(solution)/shard_map/dot_general | solution.py:182
  5.2 1.1 convolution_add_fusion
  6.3 2.8 %copy.60 = f32[4,2,16,8,32]{3,2,1,0,4:T(8,128)S(1)} copy(f32[4,2,16,8,32]{4,3,2,1,0:T(8,128)} %param.24) | data formatting | bytes 262144 | tf_op args[1]
  9.1 1.1 reshape.234
  10.2 0.5 copy.61
  11.1 1.3 pad_maximum_fusion
  12.4 6.4 %all-to-all-start = ((f32[16,36,640]{2,1,0:T(8,128)}), f32[16,36,640]{2,1,0:T(8,128)}, u32[]{:S(2)}, u32[]{:S(2)}) async-start(f32[16,36,640]{2,1,0:T(8,128)} %pad_maximum_fusion), calls=%async_computation | async-start | bytes 3276800 | tf_op jit(solution)/shard_map/all_to_all | solution.py:198
  19.2 0.8 copy-done.1
  20.1 36.2 %all-to-all-done = f32[16,36,640]{2,1,0:T(8,128)} async-done(((f32[16,36,640]{2,1,0:T(8,128)}), f32[16,36,640]{2,1,0:T(8,128)}, u32[]{:S(2)}, u32[]{:S(2)}) %all-to-all-start) | async-done | bytes 1474592 | tf_op jit(solution)/shard_map/all_to_all | solution.py:198
  56.3 1.0 slice.160
  57.4 1.4 %slice.162 = f32[16,32,640]{2,1,0:T(8,128)S(1)} slice(f32[16,36,640]{2,1,0:T(8,128)} %all-to-all-done), slice={[0:16], [0:32], [0:640]} | slice | bytes 2621440 | tf_op jit(solution)/shard_map/slice | solution.py:199
  59.7 1.4 %copy.65 = f32[16,2048]{0,1:T(8,128)} copy(f32[16,2048]{1,0:T(8,128)S(1)} %slice.163) | data formatting | bytes 262144 | tf_op jit(solution)/shard_map/slice | solution.py:202
  61.0 1.6 %copy.66 = f32[4,2,16,2,16,8]{2,5,4,3,1,0:T(8,128)S(1)} copy(f32[4,2,16,2,16,8]{4,3,5,2,1,0:T(2,128)} %bitcast.59) | data formatting | bytes 262144 | tf_op jit(solution)/shard_map/transpose | solution.py:203
  62.7 0.9 fusion.46
  63.6 1.2 copy.75
  65.7 1.0 shard_map.106
  66.7 0.7 shard_map.107
  67.7 1.4 %collective-permute-start.1 = (f32[16,2,24,128]{3,2,1,0:T(8,128)S(1)}, f32[16,2,24,128]{3,2,1,0:T(8,128)S(1)}, u32[]{:S(2)}, u32[]{:S(2)}) collective-permute-start(f32[16,2,24,128]{3,2,1,0:T(8,128)S(1)} %get-tuple-element.114), channel_id=1, source_target_pairs={{1,0},{2,1},{3,2},{4,3},{5,4},{6,5},{7,6},{8,7},{9,8},{10,9},{11,1... | collective-permute-start | bytes 1179656 | tf_op jit(solution)/shard_map/ppermute | solution.py:23
  69.2 1.0 slice.170.refs_0_
  70.1 0.5 shard_map.114
  70.9 1.5 %collective-permute-start.9 = (f32[16,2,16,128]{3,2,1,0:T(8,128)S(1)}, f32[16,2,16,128]{3,2,1,0:T(8,128)S(1)}, u32[]{:S(2)}, u32[]{:S(2)}) collective-permute-start(f32[16,2,16,128]{3,2,1,0:T(8,128)S(1)} %get-tuple-element.128), channel_id=1, source_target_pairs={{1,0},{2,1},{3,2},{4,3},{5,4},{6,5},{7,6},{8,7},{9,8},{10,9},{11,1... | collective-permute-start | bytes 786440 | tf_op jit(solution)/shard_map/ppermute | solution.py:23
  72.4 1.0 shard_map.108
  73.4 8.3 %collective-permute-done.refs_1_ = f32[16,2,24,128]{3,2,1,0:T(8,128)S(1)} collective-permute-done((f32[16,2,24,128]{3,2,1,0:T(8,128)S(1)}, f32[16,2,24,128]{3,2,1,0:T(8,128)S(1)}, u32[]{:S(2)}, u32[]{:S(2)}) %collective-permute-start) | collective-permute-done | bytes 393248 | tf_op jit(solution)/shard_map/ppermute | solution.py:23
  81.6 1.9 %collective-permute-done.1.refs_2_ = f32[16,2,24,128]{3,2,1,0:T(8,128)S(1)} collective-permute-done((f32[16,2,24,128]{3,2,1,0:T(8,128)S(1)}, f32[16,2,24,128]{3,2,1,0:T(8,128)S(1)}, u32[]{:S(2)}, u32[]{:S(2)}) %collective-permute-start.1) | collective-permute-done | bytes 393248 | tf_op jit(solution)/shard_map/ppermute | solution.py:23
  83.5 0.7 shard_map.109
  84.3 2.0 %collective-permute-start.3 = (f32[16,2,24,128]{3,2,1,0:T(8,128)S(1)}, f32[16,2,24,128]{3,2,1,0:T(8,128)S(1)}, u32[]{:S(2)}, u32[]{:S(2)}) collective-permute-start(f32[16,2,24,128]{3,2,1,0:T(8,128)S(1)} %get-tuple-element.117), channel_id=1, source_target_pairs={{1,0},{2,1},{3,2},{4,3},{5,4},{6,5},{7,6},{8,7},{9,8},{10,9},{11,1... | collective-permute-start | bytes 1179656 | tf_op jit(solution)/shard_map/ppermute | solution.py:23
  86.4 0.5 shard_map.115
  86.9 2.1 %collective-permute-start.11 = (f32[16,2,16,128]{3,2,1,0:T(8,128)S(1)}, f32[16,2,16,128]{3,2,1,0:T(8,128)S(1)}, u32[]{:S(2)}, u32[]{:S(2)}) collective-permute-start(f32[16,2,16,128]{3,2,1,0:T(8,128)S(1)} %get-tuple-element.131), channel_id=1, source_target_pairs={{1,0},{2,1},{3,2},{4,3},{5,4},{6,5},{7,6},{8,7},{9,8},{10,9},{11,1... | collective-permute-start | bytes 786440 | tf_op jit(solution)/shard_map/ppermute | solution.py:23
  89.1 1.0 shard_map.110
  90.0 11.5 %collective-permute-done.10.refs_1_ = f32[16,2,16,128]{3,2,1,0:T(8,128)S(1)} collective-permute-done((f32[16,2,16,128]{3,2,1,0:T(8,128)S(1)}, f32[16,2,16,128]{3,2,1,0:T(8,128)S(1)}, u32[]{:S(2)}, u32[]{:S(2)}) %collective-permute-start.10) | collective-permute-done | bytes 262176 | tf_op jit(solution)/shard_map/ppermute | solution.py:23
  101.5 0.5 shard_map.116
  102.1 1.7 %collective-permute-start.13 = (f32[16,2,16,128]{3,2,1,0:T(8,128)S(1)}, f32[16,2,16,128]{3,2,1,0:T(8,128)S(1)}, u32[]{:S(2)}, u32[]{:S(2)}) collective-permute-start(f32[16,2,16,128]{3,2,1,0:T(8,128)S(1)} %get-tuple-element.135), channel_id=1, source_target_pairs={{1,0},{2,1},{3,2},{4,3},{5,4},{6,5},{7,6},{8,7},{9,8},{10,9},{11,1... | collective-permute-start | bytes 786440 | tf_op jit(solution)/shard_map/ppermute | solution.py:23
  103.8 0.7 shard_map.111
  104.6 1.7 %collective-permute-start.5 = (f32[16,2,24,128]{3,2,1,0:T(8,128)S(1)}, f32[16,2,24,128]{3,2,1,0:T(8,128)S(1)}, u32[]{:S(2)}, u32[]{:S(2)}) collective-permute-start(f32[16,2,24,128]{3,2,1,0:T(8,128)S(1)} %get-tuple-element.121), channel_id=1, source_target_pairs={{1,0},{2,1},{3,2},{4,3},{5,4},{6,5},{7,6},{8,7},{9,8},{10,9},{11,1... | collective-permute-start | bytes 1179656 | tf_op jit(solution)/shard_map/ppermute | solution.py:23
  106.4 0.9 shard_map.112
  107.3 7.6 %collective-permute-done.12.refs_1_ = f32[16,2,16,128]{3,2,1,0:T(8,128)S(1)} collective-permute-done((f32[16,2,16,128]{3,2,1,0:T(8,128)S(1)}, f32[16,2,16,128]{3,2,1,0:T(8,128)S(1)}, u32[]{:S(2)}, u32[]{:S(2)}) %collective-permute-start.12) | collective-permute-done | bytes 262176 | tf_op jit(solution)/shard_map/ppermute | solution.py:23
  114.9 0.5 shard_map.117
  115.5 1.8 %collective-permute-start.15 = (f32[16,2,16,128]{3,2,1,0:T(8,128)S(1)}, f32[16,2,16,128]{3,2,1,0:T(8,128)S(1)}, u32[]{:S(2)}, u32[]{:S(2)}) collective-permute-start(f32[16,2,16,128]{3,2,1,0:T(8,128)S(1)} %get-tuple-element.139), channel_id=1, source_target_pairs={{1,0},{2,1},{3,2},{4,3},{5,4},{6,5},{7,6},{8,7},{9,8},{10,9},{11,1... | collective-permute-start | bytes 786440 | tf_op jit(solution)/shard_map/ppermute | solution.py:23
  117.3 1.8 %collective-permute-done.4.refs_1_ = f32[16,2,24,128]{3,2,1,0:T(8,128)S(1)} collective-permute-done((f32[16,2,24,128]{3,2,1,0:T(8,128)S(1)}, f32[16,2,24,128]{3,2,1,0:T(8,128)S(1)}, u32[]{:S(2)}, u32[]{:S(2)}) %collective-permute-start.4) | collective-permute-done | bytes 393248 | tf_op jit(solution)/shard_map/ppermute | solution.py:23
  119.1 0.7 shard_map.113
  119.9 1.8 %collective-permute-start.7 = (f32[16,2,24,128]{3,2,1,0:T(8,128)S(1)}, f32[16,2,24,128]{3,2,1,0:T(8,128)S(1)}, u32[]{:S(2)}, u32[]{:S(2)}) collective-permute-start(f32[16,2,24,128]{3,2,1,0:T(8,128)S(1)} %get-tuple-element.125), channel_id=1, source_target_pairs={{1,0},{2,1},{3,2},{4,3},{5,4},{6,5},{7,6},{8,7},{9,8},{10,9},{11,1... | collective-permute-start | bytes 1179656 | tf_op jit(solution)/shard_map/ppermute | solution.py:23
  121.7 7.2 %collective-permute-done.14 = f32[16,2,16,128]{3,2,1,0:T(8,128)S(1)} collective-permute-done((f32[16,2,16,128]{3,2,1,0:T(8,128)S(1)}, f32[16,2,16,128]{3,2,1,0:T(8,128)S(1)}, u32[]{:S(2)}, u32[]{:S(2)}) %collective-permute-start.14) | collective-permute-done | bytes 262176 | tf_op jit(solution)/shard_map/ppermute | solution.py:23
  129.0 4.1 %collective-permute-done.6 = f32[16,2,24,128]{3,2,1,0:T(8,128)S(1)} collective-permute-done((f32[16,2,24,128]{3,2,1,0:T(8,128)S(1)}, f32[16,2,24,128]{3,2,1,0:T(8,128)S(1)}, u32[]{:S(2)}, u32[]{:S(2)}) %collective-permute-start.6) | collective-permute-done | bytes 393248 | tf_op jit(solution)/shard_map/ppermute | solution.py:23
  133.3 1.2 copy.72
  134.5 0.6 copy.73
  (63 shorter events, 4.1 us)
Async XLA Ops:
  0.6 4.6 %copy-start.3 = (f32[256,640]{1,0:T(8,128)S(1)}, f32[256,640]{1,0:T(8,128)}, u32[]{:S(2)}) copy-start(f32[256,640]{1,0:T(8,128)} %param.26) | copy-start | bytes 1966084
  12.4 6.4 %copy-start.2 = (f32[40,16,2,128]{3,2,1,0:T(2,128)S(1)}, f32[40,16,2,128]{3,2,1,0:T(2,128)}, u32[]{:S(2)}) copy-start(f32[40,16,2,128]{3,2,1,0:T(2,128)} %param.23) | copy-start | bytes 1966084
  12.4 43.9 %all-to-all-start = ((f32[16,36,640]{2,1,0:T(8,128)}), f32[16,36,640]{2,1,0:T(8,128)}, u32[]{:S(2)}, u32[]{:S(2)}) async-start(f32[16,36,640]{2,1,0:T(8,128)} %pad_maximum_fusion), calls=%async_computation | async-start | bytes 3276800 | tf_op jit(solution)/shard_map/all_to_all | solution.py:198
  19.2 0.8 copy-start.1
  65.7 1.0 copy-start
  67.4 14.3 %collective-permute-start = (f32[16,2,24,128]{3,2,1,0:T(8,128)S(1)}, f32[16,2,24,128]{3,2,1,0:T(8,128)S(1)}, u32[]{:S(2)}, u32[]{:S(2)}) collective-permute-start(f32[16,2,24,128]{3,2,1,0:T(8,128)S(1)} %get-tuple-element.113), channel_id=1, source_target_pairs={{15,0},{0,1},{1,2},{2,3},{3,4},{4,5},{5,6},{6,7},{7,8},{8,9},{9,10... | collective-permute-start | bytes 1179656 | tf_op jit(solution)/shard_map/ppermute | solution.py:23
  67.7 15.8 %collective-permute-start.1 = (f32[16,2,24,128]{3,2,1,0:T(8,128)S(1)}, f32[16,2,24,128]{3,2,1,0:T(8,128)S(1)}, u32[]{:S(2)}, u32[]{:S(2)}) collective-permute-start(f32[16,2,24,128]{3,2,1,0:T(8,128)S(1)} %get-tuple-element.114), channel_id=1, source_target_pairs={{1,0},{2,1},{3,2},{4,3},{5,4},{6,5},{7,6},{8,7},{9,8},{10,9},{11,1... | collective-permute-start | bytes 1179656 | tf_op jit(solution)/shard_map/ppermute | solution.py:23
  70.6 15.7 %collective-permute-start.8 = (f32[16,2,16,128]{3,2,1,0:T(8,128)S(1)}, f32[16,2,16,128]{3,2,1,0:T(8,128)S(1)}, u32[]{:S(2)}, u32[]{:S(2)}) collective-permute-start(f32[16,2,16,128]{3,2,1,0:T(8,128)S(1)} %get-tuple-element.127), channel_id=1, source_target_pairs={{15,0},{0,1},{1,2},{2,3},{3,4},{4,5},{5,6},{6,7},{7,8},{8,9},{9,10... | collective-permute-start | bytes 786440 | tf_op jit(solution)/shard_map/ppermute | solution.py:23
  70.9 15.5 %collective-permute-start.9 = (f32[16,2,16,128]{3,2,1,0:T(8,128)S(1)}, f32[16,2,16,128]{3,2,1,0:T(8,128)S(1)}, u32[]{:S(2)}, u32[]{:S(2)}) collective-permute-start(f32[16,2,16,128]{3,2,1,0:T(8,128)S(1)} %get-tuple-element.128), channel_id=1, source_target_pairs={{1,0},{2,1},{3,2},{4,3},{5,4},{6,5},{7,6},{8,7},{9,8},{10,9},{11,1... | collective-permute-start | bytes 786440 | tf_op jit(solution)/shard_map/ppermute | solution.py:23
  84.3 19.6 %collective-permute-start.2 = (f32[16,2,24,128]{3,2,1,0:T(8,128)S(1)}, f32[16,2,24,128]{3,2,1,0:T(8,128)S(1)}, u32[]{:S(2)}, u32[]{:S(2)}) collective-permute-start(f32[16,2,24,128]{3,2,1,0:T(8,128)S(1)} %get-tuple-element.116), channel_id=1, source_target_pairs={{15,0},{0,1},{1,2},{2,3},{3,4},{4,5},{5,6},{6,7},{7,8},{8,9},{9,10... | collective-permute-start | bytes 1179656 | tf_op jit(solution)/shard_map/ppermute | solution.py:23
  84.3 19.5 %collective-permute-start.3 = (f32[16,2,24,128]{3,2,1,0:T(8,128)S(1)}, f32[16,2,24,128]{3,2,1,0:T(8,128)S(1)}, u32[]{:S(2)}, u32[]{:S(2)}) collective-permute-start(f32[16,2,24,128]{3,2,1,0:T(8,128)S(1)} %get-tuple-element.117), channel_id=1, source_target_pairs={{1,0},{2,1},{3,2},{4,3},{5,4},{6,5},{7,6},{8,7},{9,8},{10,9},{11,1... | collective-permute-start | bytes 1179656 | tf_op jit(solution)/shard_map/ppermute | solution.py:23
  86.9 14.7 %collective-permute-start.10 = (f32[16,2,16,128]{3,2,1,0:T(8,128)S(1)}, f32[16,2,16,128]{3,2,1,0:T(8,128)S(1)}, u32[]{:S(2)}, u32[]{:S(2)}) collective-permute-start(f32[16,2,16,128]{3,2,1,0:T(8,128)S(1)} %get-tuple-element.130), channel_id=1, source_target_pairs={{15,0},{0,1},{1,2},{2,3},{3,4},{4,5},{5,6},{6,7},{7,8},{8,9},{9,10... | collective-permute-start | bytes 786440 | tf_op jit(solution)/shard_map/ppermute | solution.py:23
  86.9 14.6 %collective-permute-start.11 = (f32[16,2,16,128]{3,2,1,0:T(8,128)S(1)}, f32[16,2,16,128]{3,2,1,0:T(8,128)S(1)}, u32[]{:S(2)}, u32[]{:S(2)}) collective-permute-start(f32[16,2,16,128]{3,2,1,0:T(8,128)S(1)} %get-tuple-element.131), channel_id=1, source_target_pairs={{1,0},{2,1},{3,2},{4,3},{5,4},{6,5},{7,6},{8,7},{9,8},{10,9},{11,1... | collective-permute-start | bytes 786440 | tf_op jit(solution)/shard_map/ppermute | solution.py:23
  102.0 12.9 %collective-permute-start.12 = (f32[16,2,16,128]{3,2,1,0:T(8,128)S(1)}, f32[16,2,16,128]{3,2,1,0:T(8,128)S(1)}, u32[]{:S(2)}, u32[]{:S(2)}) collective-permute-start(f32[16,2,16,128]{3,2,1,0:T(8,128)S(1)} %get-tuple-element.134), channel_id=1, source_target_pairs={{15,0},{0,1},{1,2},{2,3},{3,4},{4,5},{5,6},{6,7},{7,8},{8,9},{9,10... | collective-permute-start | bytes 786440 | tf_op jit(solution)/shard_map/ppermute | solution.py:23
  102.1 12.8 %collective-permute-start.13 = (f32[16,2,16,128]{3,2,1,0:T(8,128)S(1)}, f32[16,2,16,128]{3,2,1,0:T(8,128)S(1)}, u32[]{:S(2)}, u32[]{:S(2)}) collective-permute-start(f32[16,2,16,128]{3,2,1,0:T(8,128)S(1)} %get-tuple-element.135), channel_id=1, source_target_pairs={{1,0},{2,1},{3,2},{4,3},{5,4},{6,5},{7,6},{8,7},{9,8},{10,9},{11,1... | collective-permute-start | bytes 786440 | tf_op jit(solution)/shard_map/ppermute | solution.py:23
  104.6 14.5 %collective-permute-start.4 = (f32[16,2,24,128]{3,2,1,0:T(8,128)S(1)}, f32[16,2,24,128]{3,2,1,0:T(8,128)S(1)}, u32[]{:S(2)}, u32[]{:S(2)}) collective-permute-start(f32[16,2,24,128]{3,2,1,0:T(8,128)S(1)} %get-tuple-element.120), channel_id=1, source_target_pairs={{15,0},{0,1},{1,2},{2,3},{3,4},{4,5},{5,6},{6,7},{7,8},{8,9},{9,10... | collective-permute-start | bytes 1179656 | tf_op jit(solution)/shard_map/ppermute | solution.py:23
  104.6 14.5 %collective-permute-start.5 = (f32[16,2,24,128]{3,2,1,0:T(8,128)S(1)}, f32[16,2,24,128]{3,2,1,0:T(8,128)S(1)}, u32[]{:S(2)}, u32[]{:S(2)}) collective-permute-start(f32[16,2,24,128]{3,2,1,0:T(8,128)S(1)} %get-tuple-element.121), channel_id=1, source_target_pairs={{1,0},{2,1},{3,2},{4,3},{5,4},{6,5},{7,6},{8,7},{9,8},{10,9},{11,1... | collective-permute-start | bytes 1179656 | tf_op jit(solution)/shard_map/ppermute | solution.py:23
  115.4 13.5 %collective-permute-start.14 = (f32[16,2,16,128]{3,2,1,0:T(8,128)S(1)}, f32[16,2,16,128]{3,2,1,0:T(8,128)S(1)}, u32[]{:S(2)}, u32[]{:S(2)}) collective-permute-start(f32[16,2,16,128]{3,2,1,0:T(8,128)S(1)} %get-tuple-element.138), channel_id=1, source_target_pairs={{15,0},{0,1},{1,2},{2,3},{3,4},{4,5},{5,6},{6,7},{7,8},{8,9},{9,10... | collective-permute-start | bytes 786440 | tf_op jit(solution)/shard_map/ppermute | solution.py:23
  115.5 13.5 %collective-permute-start.15 = (f32[16,2,16,128]{3,2,1,0:T(8,128)S(1)}, f32[16,2,16,128]{3,2,1,0:T(8,128)S(1)}, u32[]{:S(2)}, u32[]{:S(2)}) collective-permute-start(f32[16,2,16,128]{3,2,1,0:T(8,128)S(1)} %get-tuple-element.139), channel_id=1, source_target_pairs={{1,0},{2,1},{3,2},{4,3},{5,4},{6,5},{7,6},{8,7},{9,8},{10,9},{11,1... | collective-permute-start | bytes 786440 | tf_op jit(solution)/shard_map/ppermute | solution.py:23
  119.8 13.3 %collective-permute-start.6 = (f32[16,2,24,128]{3,2,1,0:T(8,128)S(1)}, f32[16,2,24,128]{3,2,1,0:T(8,128)S(1)}, u32[]{:S(2)}, u32[]{:S(2)}) collective-permute-start(f32[16,2,24,128]{3,2,1,0:T(8,128)S(1)} %get-tuple-element.124), channel_id=1, source_target_pairs={{15,0},{0,1},{1,2},{2,3},{3,4},{4,5},{5,6},{6,7},{7,8},{8,9},{9,10... | collective-permute-start | bytes 1179656 | tf_op jit(solution)/shard_map/ppermute | solution.py:23
  119.9 13.3 %collective-permute-start.7 = (f32[16,2,24,128]{3,2,1,0:T(8,128)S(1)}, f32[16,2,24,128]{3,2,1,0:T(8,128)S(1)}, u32[]{:S(2)}, u32[]{:S(2)}) collective-permute-start(f32[16,2,24,128]{3,2,1,0:T(8,128)S(1)} %get-tuple-element.125), channel_id=1, source_target_pairs={{1,0},{2,1},{3,2},{4,3},{5,4},{6,5},{7,6},{8,7},{9,8},{10,9},{11,1... | collective-permute-start | bytes 1179656 | tf_op jit(solution)/shard_map/ppermute | solution.py:23

commit v3 on v1

--- a/solution.py
+++ b/solution.py
@@ -188,8 +188,9 @@
     small = jnp.concatenate(
         [parts.reshape(bands, -1), send_code.reshape(bands, capacity)], axis=1
     )
+    recv_values = lax.all_to_all(send_values, "lon", split_axis=0, concat_axis=0, tiled=True)
+    recv_values, small = lax.optimization_barrier((recv_values, small))
     small = lax.all_to_all(small, "lon", split_axis=0, concat_axis=0, tiled=True)
-    recv_values = lax.all_to_all(send_values, "lon", split_axis=0, concat_axis=0, tiled=True)
     recv_code = small[:, -capacity:].reshape(-1).astype(jnp.int32)
     own = small[:, :-capacity].reshape(bands, steps, 2, levels, lat_rows, columns)
     own = own.transpose(1, 2, 3, 5, 0, 4).reshape(steps, 2, levels, columns, lat)

time: 131 us -> 132 us (level)
  waiting for transfers between devices: 66.4 us -> 71.2 us
  other arithmetic: 3.99 us -> 1.93 us
  starting transfers between devices: 28.1 us -> 26.5 us
    all_to_all x1, waiting for transfers between devices: 0.54 us -> 4.35 us  [body(): lax.all_to_all(small, 'lon', split_axis=0, concat_axis=0, tiled=True)]
    reshape x1, local copies, waits for them, and re-layouts: 1.07 us -> 2.71 us  [body(): winds.reshape(steps * 2 * levels * lat_rows, bands, columns)]
    all_to_all x1 -> x0, local copies, waits for them, and re-layouts: 1.48 us -> none  [body(): lax.all_to_all(send_values, 'lon', split_axis=0, concat_axis=0, tiled=True)]
    ppermute x16, waiting for transfers between devices: 43 us -> 44.4 us  [shifted(): return lax.ppermute(block, axis, route)]
    unnamed x15 -> x21, local copies, waits for them, and re-layouts: 8.28 us -> 7.26 us
  transfers between devices with their start and end apart: 18 -> 18, of which waited for: 9 -> 10; matrix products, arithmetic and copies ran while one was open for 9% -> 7% of each run, Pallas kernels for 5% -> 5%
where the time goes in v3:
time: 132 us
  waiting for transfers between devices  71.2 us (54%)
  starting transfers between devices  26.5 us (20%)
  local copies, waits for them, and re-layouts  17.2 us (13%)
  Pallas kernels  8.6 us (7%)
  matrix products  5.09 us (4%)
  other arithmetic  1.93 us (1%)
    ppermute x16, waiting for transfers between devices, shifted(): return lax.ppermute(block, axis, route)  44.4 us
    all_to_all x1, waiting for transfers between devices, body(): lax.all_to_all(send_values, 'lon', split_axis=0, concat_axis=0, tiled=True)  22.4 us
    ppermute x16, starting transfers between devices, shifted(): return lax.ppermute(block, axis, route)  15.1 us
    unnamed x21, local copies, waits for them, and re-layouts  7.26 us
    all_to_all x1, starting transfers between devices, body(): lax.all_to_all(send_values, 'lon', split_axis=0, concat_axis=0, tiled=True)  6.37 us
    all_to_all x1, starting transfers between devices, body(): lax.all_to_all(small, 'lon', split_axis=0, concat_axis=0, tiled=True)  5.01 us
    pallas_call x8, Pallas kernels, step(): pl.pallas_call(functools.partial(step_kernel, bool(halos), start), out_sh...  4.8 us
    all_to_all x1, waiting for transfers between devices, body(): lax.all_to_all(small, 'lon', split_axis=0, concat_axis=0, tiled=True)  4.35 us
  transfers between devices with their start and end apart: 18, of which 10 were waited for; matrix products, arithmetic and copies ran while one was open for 7% of the time, Pallas kernels for 5%

profile of v3, /device:TPU:12, one launch (start us, length us, event | category | flops | bytes accessed | tf_op | source)
XLA Modules:
  0.0 131.5 jit_solution(9192367094709510955)
XLA Ops:
  0.7 1.0 fusion.5
  1.6 0.7 multiply_add_fusion
  2.3 1.9 %fusion.4 = f32[512,640]{1,0:T(8,128)S(1)} fusion(s32[640]{0:T(1024)S(1)} %fusion.43, f32[256,640]{1,0:T(8,128)} %param.26, s32[256]{0:T(256)S(1)} %bitcast.65), kind=kOutput, calls=%fused_computation.9 | convolution fusion | flops 378683392 | bytes 1969664 | tf_op jit(solution)/shard_map/dot_general | solution.py:182
  4.3 2.2 %convolution_add_fusion = f32[512,640]{1,0:T(8,128)} fusion(f32[512,640]{1,0:T(8,128)S(1)} %fusion.4, s32[640]{0:T(1024)S(1)} %fusion.43, f32[256,640]{1,0:T(8,128)S(1)} %copy-done.3, s32[256]{0:T(256)S(1)} %bitcast.66), kind=kOutput, calls=%fused_computation.5 | convolution fusion | flops 379387904 | bytes 3280384 | tf_op jit(solution)/shard_map/dot_general | solution.py:182
  6.5 6.4 %all-to-all-start = ((f32[16,32,640]{2,1,0:T(8,128)}), f32[16,32,640]{2,1,0:T(8,128)S(1)}, u32[]{:S(2)}, u32[]{:S(2)}) async-start(f32[16,32,640]{2,1,0:T(8,128)} %bitcast.4), calls=%async_computation | async-start | bytes 2621440 | tf_op jit(solution)/shard_map/all_to_all | solution.py:191
  13.5 0.8 copy-done.1
  14.4 2.8 %copy.76 = f32[4,2,16,8,32]{3,2,1,0,4:T(8,128)} copy(f32[4,2,16,8,32]{4,3,2,1,0:T(8,128)S(1)} %copy-done.4) | data formatting | bytes 262144 | tf_op args[1]
  17.2 2.7 %reshape.225 = f32[1024,16,2]{0,2,1:T(2,128)S(1)} reshape(f32[4,2,16,8,32]{3,2,1,0,4:T(8,128)} %copy.76) | data formatting | bytes 262144 | tf_op jit(solution)/shard_map/reshape | solution.py:187
  19.9 0.5 copy.77
  20.8 22.4 %all-to-all-done = f32[16,32,640]{2,1,0:T(8,128)S(1)} async-done(((f32[16,32,640]{2,1,0:T(8,128)}), f32[16,32,640]{2,1,0:T(8,128)S(1)}, u32[]{:S(2)}, u32[]{:S(2)}) %all-to-all-start) | async-done | bytes 1310752 | tf_op jit(solution)/shard_map/all_to_all | solution.py:191
  43.3 0.7 all_to_all.19
  44.0 5.0 %all-to-all-start.1 = ((f32[16,1,2080]{2,1,0:T(1,128)}), f32[16,1,2080]{2,1,0:T(1,128)S(1)}, u32[]{:S(2)}, u32[]{:S(2)}) async-start(f32[16,1,2080]{2,1,0:T(1,128)} %all_to_all.19), calls=%async_computation.1 | async-start | bytes 278528 | tf_op jit(solution)/shard_map/all_to_all | solution.py:193
  49.6 4.3 %all-to-all-done.1 = f32[16,1,2080]{2,1,0:T(1,128)S(1)} async-done(((f32[16,1,2080]{2,1,0:T(1,128)}), f32[16,1,2080]{2,1,0:T(1,128)S(1)}, u32[]{:S(2)}, u32[]{:S(2)}) %all-to-all-start.1) | async-done | bytes 133152 | tf_op jit(solution)/shard_map/all_to_all | solution.py:193
  54.3 1.3 %copy.81 = f32[16,2048]{0,1:T(8,128)} copy(f32[16,2048]{1,0:T(8,128)S(1)} %slice.150) | data formatting | bytes 262144 | tf_op jit(solution)/shard_map/slice | solution.py:195
  55.6 1.6 %copy.82 = f32[4,2,16,2,16,8]{2,5,4,3,1,0:T(8,128)S(1)} copy(f32[4,2,16,2,16,8]{4,3,5,2,1,0:T(2,128)} %bitcast.59) | data formatting | bytes 262144 | tf_op jit(solution)/shard_map/transpose | solution.py:196
  57.2 0.9 fusion.46
  58.1 1.2 copy.92
  60.3 1.0 shard_map.106
  61.2 0.7 shard_map.107
  61.9 0.6 collective-permute-start
  62.5 1.2 collective-permute-start.1
  63.7 1.0 slice.157.refs_0_
  65.2 0.6 collective-permute-start.8
  65.8 1.2 collective-permute-start.9
  67.0 0.9 shard_map.108
  67.9 8.3 %collective-permute-done.refs_1_ = f32[16,2,24,128]{3,2,1,0:T(8,128)S(1)} collective-permute-done((f32[16,2,24,128]{3,2,1,0:T(8,128)S(1)}, f32[16,2,24,128]{3,2,1,0:T(8,128)S(1)}, u32[]{:S(2)}, u32[]{:S(2)}) %collective-permute-start) | collective-permute-done | bytes 393248 | tf_op jit(solution)/shard_map/ppermute | solution.py:23
  76.2 3.7 %collective-permute-done.1.refs_2_ = f32[16,2,24,128]{3,2,1,0:T(8,128)S(1)} collective-permute-done((f32[16,2,24,128]{3,2,1,0:T(8,128)S(1)}, f32[16,2,24,128]{3,2,1,0:T(8,128)S(1)}, u32[]{:S(2)}, u32[]{:S(2)}) %collective-permute-start.1) | collective-permute-done | bytes 393248 | tf_op jit(solution)/shard_map/ppermute | solution.py:23
  80.0 0.7 shard_map.109
  80.8 2.0 %collective-permute-start.3 = (f32[16,2,24,128]{3,2,1,0:T(8,128)S(1)}, f32[16,2,24,128]{3,2,1,0:T(8,128)S(1)}, u32[]{:S(2)}, u32[]{:S(2)}) collective-permute-start(f32[16,2,24,128]{3,2,1,0:T(8,128)S(1)} %get-tuple-element.121), channel_id=1, source_target_pairs={{1,0},{2,1},{3,2},{4,3},{5,4},{6,5},{7,6},{8,7},{9,8},{10,9},{11,1... | collective-permute-start | bytes 1179656 | tf_op jit(solution)/shard_map/ppermute | solution.py:23
  82.8 0.5 shard_map.115
  83.3 2.1 %collective-permute-start.11 = (f32[16,2,16,128]{3,2,1,0:T(8,128)S(1)}, f32[16,2,16,128]{3,2,1,0:T(8,128)S(1)}, u32[]{:S(2)}, u32[]{:S(2)}) collective-permute-start(f32[16,2,16,128]{3,2,1,0:T(8,128)S(1)} %get-tuple-element.135), channel_id=1, source_target_pairs={{1,0},{2,1},{3,2},{4,3},{5,4},{6,5},{7,6},{8,7},{9,8},{10,9},{11,1... | collective-permute-start | bytes 786440 | tf_op jit(solution)/shard_map/ppermute | solution.py:23
  85.5 1.0 shard_map.110
  86.5 11.5 %collective-permute-done.10.refs_1_ = f32[16,2,16,128]{3,2,1,0:T(8,128)S(1)} collective-permute-done((f32[16,2,16,128]{3,2,1,0:T(8,128)S(1)}, f32[16,2,16,128]{3,2,1,0:T(8,128)S(1)}, u32[]{:S(2)}, u32[]{:S(2)}) %collective-permute-start.10) | collective-permute-done | bytes 262176 | tf_op jit(solution)/shard_map/ppermute | solution.py:23
  98.0 0.5 shard_map.116
  98.5 1.7 %collective-permute-start.13 = (f32[16,2,16,128]{3,2,1,0:T(8,128)S(1)}, f32[16,2,16,128]{3,2,1,0:T(8,128)S(1)}, u32[]{:S(2)}, u32[]{:S(2)}) collective-permute-start(f32[16,2,16,128]{3,2,1,0:T(8,128)S(1)} %get-tuple-element.139), channel_id=1, source_target_pairs={{1,0},{2,1},{3,2},{4,3},{5,4},{6,5},{7,6},{8,7},{9,8},{10,9},{11,1... | collective-permute-start | bytes 786440 | tf_op jit(solution)/shard_map/ppermute | solution.py:23
  100.3 0.7 shard_map.111
  101.1 1.7 %collective-permute-start.5 = (f32[16,2,24,128]{3,2,1,0:T(8,128)S(1)}, f32[16,2,24,128]{3,2,1,0:T(8,128)S(1)}, u32[]{:S(2)}, u32[]{:S(2)}) collective-permute-start(f32[16,2,24,128]{3,2,1,0:T(8,128)S(1)} %get-tuple-element.125), channel_id=1, source_target_pairs={{1,0},{2,1},{3,2},{4,3},{5,4},{6,5},{7,6},{8,7},{9,8},{10,9},{11,1... | collective-permute-start | bytes 1179656 | tf_op jit(solution)/shard_map/ppermute | solution.py:23
  102.8 0.9 shard_map.112
  103.7 7.6 %collective-permute-done.12.refs_1_ = f32[16,2,16,128]{3,2,1,0:T(8,128)S(1)} collective-permute-done((f32[16,2,16,128]{3,2,1,0:T(8,128)S(1)}, f32[16,2,16,128]{3,2,1,0:T(8,128)S(1)}, u32[]{:S(2)}, u32[]{:S(2)}) %collective-permute-start.12) | collective-permute-done | bytes 262176 | tf_op jit(solution)/shard_map/ppermute | solution.py:23
  111.3 0.5 shard_map.117
  111.9 1.8 %collective-permute-start.15 = (f32[16,2,16,128]{3,2,1,0:T(8,128)S(1)}, f32[16,2,16,128]{3,2,1,0:T(8,128)S(1)}, u32[]{:S(2)}, u32[]{:S(2)}) collective-permute-start(f32[16,2,16,128]{3,2,1,0:T(8,128)S(1)} %get-tuple-element.143), channel_id=1, source_target_pairs={{1,0},{2,1},{3,2},{4,3},{5,4},{6,5},{7,6},{8,7},{9,8},{10,9},{11,1... | collective-permute-start | bytes 786440 | tf_op jit(solution)/shard_map/ppermute | solution.py:23
  113.7 1.8 %collective-permute-done.4.refs_1_ = f32[16,2,24,128]{3,2,1,0:T(8,128)S(1)} collective-permute-done((f32[16,2,24,128]{3,2,1,0:T(8,128)S(1)}, f32[16,2,24,128]{3,2,1,0:T(8,128)S(1)}, u32[]{:S(2)}, u32[]{:S(2)}) %collective-permute-start.4) | collective-permute-done | bytes 393248 | tf_op jit(solution)/shard_map/ppermute | solution.py:23
  115.5 0.7 shard_map.113
  116.3 1.8 %collective-permute-start.7 = (f32[16,2,24,128]{3,2,1,0:T(8,128)S(1)}, f32[16,2,24,128]{3,2,1,0:T(8,128)S(1)}, u32[]{:S(2)}, u32[]{:S(2)}) collective-permute-start(f32[16,2,24,128]{3,2,1,0:T(8,128)S(1)} %get-tuple-element.129), channel_id=1, source_target_pairs={{1,0},{2,1},{3,2},{4,3},{5,4},{6,5},{7,6},{8,7},{9,8},{10,9},{11,1... | collective-permute-start | bytes 1179656 | tf_op jit(solution)/shard_map/ppermute | solution.py:23
  118.1 7.2 %collective-permute-done.14 = f32[16,2,16,128]{3,2,1,0:T(8,128)S(1)} collective-permute-done((f32[16,2,16,128]{3,2,1,0:T(8,128)S(1)}, f32[16,2,16,128]{3,2,1,0:T(8,128)S(1)}, u32[]{:S(2)}, u32[]{:S(2)}) %collective-permute-start.14) | collective-permute-done | bytes 262176 | tf_op jit(solution)/shard_map/ppermute | solution.py:23
  125.4 4.1 %collective-permute-done.6 = f32[16,2,24,128]{3,2,1,0:T(8,128)S(1)} collective-permute-done((f32[16,2,24,128]{3,2,1,0:T(8,128)S(1)}, f32[16,2,24,128]{3,2,1,0:T(8,128)S(1)}, u32[]{:S(2)}, u32[]{:S(2)}) %collective-permute-start.6) | collective-permute-done | bytes 393248 | tf_op jit(solution)/shard_map/ppermute | solution.py:23
  129.7 1.2 copy.88
  130.9 0.6 copy.89
  (68 shorter events, 3.9 us)
Async XLA Ops:
  0.6 3.6 %copy-start.3 = (f32[256,640]{1,0:T(8,128)S(1)}, f32[256,640]{1,0:T(8,128)}, u32[]{:S(2)}) copy-start(f32[256,640]{1,0:T(8,128)} %param.26) | copy-start | bytes 1966084
  6.5 6.4 %copy-start.5 = (s32[256]{0:T(256)S(1)}, s32[256]{0:T(256)}, u32[]{:S(2)}) copy-start(s32[256]{0:T(256)} %param.28) | copy-start | bytes 3076
  6.5 6.4 %copy-start.6 = (s32[256]{0:T(256)S(1)}, s32[256]{0:T(256)}, u32[]{:S(2)}) copy-start(s32[256]{0:T(256)} %param.29) | copy-start | bytes 3076
  6.5 6.7 %copy-start.2 = (f32[40,16,2,128]{3,2,1,0:T(2,128)S(1)}, f32[40,16,2,128]{3,2,1,0:T(2,128)}, u32[]{:S(2)}) copy-start(f32[40,16,2,128]{3,2,1,0:T(2,128)} %param.23) | copy-start | bytes 1966084
  6.5 36.8 %all-to-all-start = ((f32[16,32,640]{2,1,0:T(8,128)}), f32[16,32,640]{2,1,0:T(8,128)S(1)}, u32[]{:S(2)}, u32[]{:S(2)}) async-start(f32[16,32,640]{2,1,0:T(8,128)} %bitcast.4), calls=%async_computation | async-start | bytes 2621440 | tf_op jit(solution)/shard_map/all_to_all | solution.py:191
  12.9 1.5 %copy-start.4 = (f32[4,2,16,8,32]{4,3,2,1,0:T(8,128)S(1)}, f32[4,2,16,8,32]{4,3,2,1,0:T(8,128)}, u32[]{:S(2)}) copy-start(f32[4,2,16,8,32]{4,3,2,1,0:T(8,128)} %param.24) | copy-start | bytes 393220
  13.5 0.8 copy-start.1
  44.0 10.0 %all-to-all-start.1 = ((f32[16,1,2080]{2,1,0:T(1,128)}), f32[16,1,2080]{2,1,0:T(1,128)S(1)}, u32[]{:S(2)}, u32[]{:S(2)}) async-start(f32[16,1,2080]{2,1,0:T(1,128)} %all_to_all.19), calls=%async_computation.1 | async-start | bytes 278528 | tf_op jit(solution)/shard_map/all_to_all | solution.py:193
  60.3 1.0 copy-start
  61.9 14.3 %collective-permute-start = (f32[16,2,24,128]{3,2,1,0:T(8,128)S(1)}, f32[16,2,24,128]{3,2,1,0:T(8,128)S(1)}, u32[]{:S(2)}, u32[]{:S(2)}) collective-permute-start(f32[16,2,24,128]{3,2,1,0:T(8,128)S(1)} %get-tuple-element.117), channel_id=1, source_target_pairs={{15,0},{0,1},{1,2},{2,3},{3,4},{4,5},{5,6},{6,7},{7,8},{8,9},{9,10... | collective-permute-start | bytes 1179656 | tf_op jit(solution)/shard_map/ppermute | solution.py:23
  62.5 17.5 %collective-permute-start.1 = (f32[16,2,24,128]{3,2,1,0:T(8,128)S(1)}, f32[16,2,24,128]{3,2,1,0:T(8,128)S(1)}, u32[]{:S(2)}, u32[]{:S(2)}) collective-permute-start(f32[16,2,24,128]{3,2,1,0:T(8,128)S(1)} %get-tuple-element.118), channel_id=1, source_target_pairs={{1,0},{2,1},{3,2},{4,3},{5,4},{6,5},{7,6},{8,7},{9,8},{10,9},{11,1... | collective-permute-start | bytes 1179656 | tf_op jit(solution)/shard_map/ppermute | solution.py:23
  65.2 17.5 %collective-permute-start.8 = (f32[16,2,16,128]{3,2,1,0:T(8,128)S(1)}, f32[16,2,16,128]{3,2,1,0:T(8,128)S(1)}, u32[]{:S(2)}, u32[]{:S(2)}) collective-permute-start(f32[16,2,16,128]{3,2,1,0:T(8,128)S(1)} %get-tuple-element.131), channel_id=1, source_target_pairs={{15,0},{0,1},{1,2},{2,3},{3,4},{4,5},{5,6},{6,7},{7,8},{8,9},{9,10... | collective-permute-start | bytes 786440 | tf_op jit(solution)/shard_map/ppermute | solution.py:23
  65.8 16.9 %collective-permute-start.9 = (f32[16,2,16,128]{3,2,1,0:T(8,128)S(1)}, f32[16,2,16,128]{3,2,1,0:T(8,128)S(1)}, u32[]{:S(2)}, u32[]{:S(2)}) collective-permute-start(f32[16,2,16,128]{3,2,1,0:T(8,128)S(1)} %get-tuple-element.132), channel_id=1, source_target_pairs={{1,0},{2,1},{3,2},{4,3},{5,4},{6,5},{7,6},{8,7},{9,8},{10,9},{11,1... | collective-permute-start | bytes 786440 | tf_op jit(solution)/shard_map/ppermute | solution.py:23
  80.7 19.6 %collective-permute-start.2 = (f32[16,2,24,128]{3,2,1,0:T(8,128)S(1)}, f32[16,2,24,128]{3,2,1,0:T(8,128)S(1)}, u32[]{:S(2)}, u32[]{:S(2)}) collective-permute-start(f32[16,2,24,128]{3,2,1,0:T(8,128)S(1)} %get-tuple-element.120), channel_id=1, source_target_pairs={{15,0},{0,1},{1,2},{2,3},{3,4},{4,5},{5,6},{6,7},{7,8},{8,9},{9,10... | collective-permute-start | bytes 1179656 | tf_op jit(solution)/shard_map/ppermute | solution.py:23
  80.8 19.5 %collective-permute-start.3 = (f32[16,2,24,128]{3,2,1,0:T(8,128)S(1)}, f32[16,2,24,128]{3,2,1,0:T(8,128)S(1)}, u32[]{:S(2)}, u32[]{:S(2)}) collective-permute-start(f32[16,2,24,128]{3,2,1,0:T(8,128)S(1)} %get-tuple-element.121), channel_id=1, source_target_pairs={{1,0},{2,1},{3,2},{4,3},{5,4},{6,5},{7,6},{8,7},{9,8},{10,9},{11,1... | collective-permute-start | bytes 1179656 | tf_op jit(solution)/shard_map/ppermute | solution.py:23
  83.3 14.7 %collective-permute-start.10 = (f32[16,2,16,128]{3,2,1,0:T(8,128)S(1)}, f32[16,2,16,128]{3,2,1,0:T(8,128)S(1)}, u32[]{:S(2)}, u32[]{:S(2)}) collective-permute-start(f32[16,2,16,128]{3,2,1,0:T(8,128)S(1)} %get-tuple-element.134), channel_id=1, source_target_pairs={{15,0},{0,1},{1,2},{2,3},{3,4},{4,5},{5,6},{6,7},{7,8},{8,9},{9,10... | collective-permute-start | bytes 786440 | tf_op jit(solution)/shard_map/ppermute | solution.py:23
  83.3 14.6 %collective-permute-start.11 = (f32[16,2,16,128]{3,2,1,0:T(8,128)S(1)}, f32[16,2,16,128]{3,2,1,0:T(8,128)S(1)}, u32[]{:S(2)}, u32[]{:S(2)}) collective-permute-start(f32[16,2,16,128]{3,2,1,0:T(8,128)S(1)} %get-tuple-element.135), channel_id=1, source_target_pairs={{1,0},{2,1},{3,2},{4,3},{5,4},{6,5},{7,6},{8,7},{9,8},{10,9},{11,1... | collective-permute-start | bytes 786440 | tf_op jit(solution)/shard_map/ppermute | solution.py:23
  98.5 12.9 %collective-permute-start.12 = (f32[16,2,16,128]{3,2,1,0:T(8,128)S(1)}, f32[16,2,16,128]{3,2,1,0:T(8,128)S(1)}, u32[]{:S(2)}, u32[]{:S(2)}) collective-permute-start(f32[16,2,16,128]{3,2,1,0:T(8,128)S(1)} %get-tuple-element.138), channel_id=1, source_target_pairs={{15,0},{0,1},{1,2},{2,3},{3,4},{4,5},{5,6},{6,7},{7,8},{8,9},{9,10... | collective-permute-start | bytes 786440 | tf_op jit(solution)/shard_map/ppermute | solution.py:23
  98.5 12.8 %collective-permute-start.13 = (f32[16,2,16,128]{3,2,1,0:T(8,128)S(1)}, f32[16,2,16,128]{3,2,1,0:T(8,128)S(1)}, u32[]{:S(2)}, u32[]{:S(2)}) collective-permute-start(f32[16,2,16,128]{3,2,1,0:T(8,128)S(1)} %get-tuple-element.139), channel_id=1, source_target_pairs={{1,0},{2,1},{3,2},{4,3},{5,4},{6,5},{7,6},{8,7},{9,8},{10,9},{11,1... | collective-permute-start | bytes 786440 | tf_op jit(solution)/shard_map/ppermute | solution.py:23
  101.0 14.5 %collective-permute-start.4 = (f32[16,2,24,128]{3,2,1,0:T(8,128)S(1)}, f32[16,2,24,128]{3,2,1,0:T(8,128)S(1)}, u32[]{:S(2)}, u32[]{:S(2)}) collective-permute-start(f32[16,2,24,128]{3,2,1,0:T(8,128)S(1)} %get-tuple-element.124), channel_id=1, source_target_pairs={{15,0},{0,1},{1,2},{2,3},{3,4},{4,5},{5,6},{6,7},{7,8},{8,9},{9,10... | collective-permute-start | bytes 1179656 | tf_op jit(solution)/shard_map/ppermute | solution.py:23
  101.1 14.5 %collective-permute-start.5 = (f32[16,2,24,128]{3,2,1,0:T(8,128)S(1)}, f32[16,2,24,128]{3,2,1,0:T(8,128)S(1)}, u32[]{:S(2)}, u32[]{:S(2)}) collective-permute-start(f32[16,2,24,128]{3,2,1,0:T(8,128)S(1)} %get-tuple-element.125), channel_id=1, source_target_pairs={{1,0},{2,1},{3,2},{4,3},{5,4},{6,5},{7,6},{8,7},{9,8},{10,9},{11,1... | collective-permute-start | bytes 1179656 | tf_op jit(solution)/shard_map/ppermute | solution.py:23
  111.8 13.5 %collective-permute-start.14 = (f32[16,2,16,128]{3,2,1,0:T(8,128)S(1)}, f32[16,2,16,128]{3,2,1,0:T(8,128)S(1)}, u32[]{:S(2)}, u32[]{:S(2)}) collective-permute-start(f32[16,2,16,128]{3,2,1,0:T(8,128)S(1)} %get-tuple-element.142), channel_id=1, source_target_pairs={{15,0},{0,1},{1,2},{2,3},{3,4},{4,5},{5,6},{6,7},{7,8},{8,9},{9,10... | collective-permute-start | bytes 786440 | tf_op jit(solution)/shard_map/ppermute | solution.py:23
  111.9 13.5 %collective-permute-start.15 = (f32[16,2,16,128]{3,2,1,0:T(8,128)S(1)}, f32[16,2,16,128]{3,2,1,0:T(8,128)S(1)}, u32[]{:S(2)}, u32[]{:S(2)}) collective-permute-start(f32[16,2,16,128]{3,2,1,0:T(8,128)S(1)} %get-tuple-element.143), channel_id=1, source_target_pairs={{1,0},{2,1},{3,2},{4,3},{5,4},{6,5},{7,6},{8,7},{9,8},{10,9},{11,1... | collective-permute-start | bytes 786440 | tf_op jit(solution)/shard_map/ppermute | solution.py:23
  116.3 13.3 %collective-permute-start.6 = (f32[16,2,24,128]{3,2,1,0:T(8,128)S(1)}, f32[16,2,24,128]{3,2,1,0:T(8,128)S(1)}, u32[]{:S(2)}, u32[]{:S(2)}) collective-permute-start(f32[16,2,24,128]{3,2,1,0:T(8,128)S(1)} %get-tuple-element.128), channel_id=1, source_target_pairs={{15,0},{0,1},{1,2},{2,3},{3,4},{4,5},{5,6},{6,7},{7,8},{8,9},{9,10... | collective-permute-start | bytes 1179656 | tf_op jit(solution)/shard_map/ppermute | solution.py:23
  116.3 13.3 %collective-permute-start.7 = (f32[16,2,24,128]{3,2,1,0:T(8,128)S(1)}, f32[16,2,24,128]{3,2,1,0:T(8,128)S(1)}, u32[]{:S(2)}, u32[]{:S(2)}) collective-permute-start(f32[16,2,24,128]{3,2,1,0:T(8,128)S(1)} %get-tuple-element.129), channel_id=1, source_target_pairs={{1,0},{2,1},{3,2},{4,3},{5,4},{6,5},{7,6},{8,7},{9,8},{10,9},{11,1... | collective-permute-start | bytes 1179656 | tf_op jit(solution)/shard_map/ppermute | solution.py:23

commit v4 on v1

--- a/solution.py
+++ b/solution.py
@@ -13,8 +13,8 @@
 
 def chunk_sizes(tracers):
     units = tracers // ROWS
-    first = (units + 1) // 2
-    return [n * ROWS for n in (first, units - first) if n]
+    return [units * ROWS * (i + 1) // 3 // ROWS * ROWS - units * ROWS * i // 3 // ROWS * ROWS
+            for i in range(3)]
 
 
 def shifted(block, axis, distance):

time: 131 us -> 136 us (1.038)
  starting transfers between devices: 28.1 us -> 33.1 us
    ppermute x16 -> x24, starting transfers between devices: 15.1 us -> 20.1 us  [shifted(): return lax.ppermute(block, axis, route)]
    unnamed x15 -> x13, local copies, waits for them, and re-layouts: 8.28 us -> 6.46 us
    ppermute x16 -> x24, waiting for transfers between devices: 43 us -> 43.8 us  [shifted(): return lax.ppermute(block, axis, route)]
    pallas_call x8 -> x12, Pallas kernels: 4.8 us -> 4.81 us  [step(): pl.pallas_call(functools.partial(step_kernel, bool(halos), start), out_sh...]
  transfers between devices with their start and end apart: 18 -> 26, of which waited for: 9 -> 9; matrix products, arithmetic and copies ran while one was open for 9% -> 9% of each run, Pallas kernels for 5% -> 5%
where the time goes in v4:
time: 136 us; the launch traced here: 135 us
  waiting for transfers between devices  67.3 us (49%)
  starting transfers between devices  33.1 us (24%)
  local copies, waits for them, and re-layouts  16.8 us (12%)
  Pallas kernels  8.62 us (6%)
  matrix products  4.02 us (3%)
  other arithmetic  3.97 us (3%)
    ppermute x24, waiting for transfers between devices, shifted(): return lax.ppermute(block, axis, route)  43.8 us
    all_to_all x1, waiting for transfers between devices, body(): lax.all_to_all(send_values, 'lon', split_axis=0, concat_axis=0, tiled=True)  22.2 us
    ppermute x24, starting transfers between devices, shifted(): return lax.ppermute(block, axis, route)  20.1 us
    all_to_all x1, starting transfers between devices, body(): lax.all_to_all(send_values, 'lon', split_axis=0, concat_axis=0, tiled=True)  6.73 us
    unnamed x13, local copies, waits for them, and re-layouts  6.46 us
    all_to_all x1, starting transfers between devices, body(): lax.all_to_all(small, 'lon', split_axis=0, concat_axis=0, tiled=True)  6.24 us
    pallas_call x12, Pallas kernels, step(): pl.pallas_call(functools.partial(step_kernel, bool(halos), start), out_sh...  4.81 us
    pallas_call x4, Pallas kernels, step_forcing(): pl.pallas_call(functools.partial(forcing_kernel, first), out_shape=jax.Sh...  3.81 us
  transfers between devices with their start and end apart: 26, of which 9 were waited for; matrix products, arithmetic and copies ran while one was open for 9% of the time, Pallas kernels for 5%

profile of v4, /device:TPU:12, one launch (start us, length us, event | category | flops | bytes accessed | tf_op | source)
XLA Modules:
  0.0 135.0 jit_solution(2229332123409695471)
XLA Ops:
  0.6 1.0 fusion.5
  1.6 0.7 multiply_add_fusion
  2.3 0.7 convert_add_fusion
  3.2 2.8 %copy.76 = f32[4,2,16,8,32]{3,2,1,0,4:T(8,128)S(1)} copy(f32[4,2,16,8,32]{4,3,2,1,0:T(8,128)} %param.32) | data formatting | bytes 262144 | tf_op args[1]
  6.1 1.1 reshape.299
  7.2 0.5 copy.77
  8.0 0.8 all_to_all.16
  8.8 6.2 %all-to-all-start = ((f32[16,1,2080]{2,1,0:T(1,128)}), f32[16,1,2080]{2,1,0:T(1,128)S(1)}, u32[]{:S(2)}, u32[]{:S(2)}) async-start(f32[16,1,2080]{2,1,0:T(1,128)} %all_to_all.16), calls=%async_computation | async-start | bytes 278528 | tf_op jit(solution)/shard_map/all_to_all | solution.py:191
  15.1 0.8 fusion.4
  15.9 2.2 %convolution_add_fusion = f32[512,640]{1,0:T(8,128)} fusion(f32[512,640]{1,0:T(8,128)S(1)} %fusion.4, s32[640]{0:T(1024)S(1)} %fusion.44, f32[256,640]{1,0:T(8,128)S(1)} %copy-done.2, s32[256]{0:T(256)S(1)} %bitcast.75), kind=kOutput, calls=%fused_computation.5 | convolution fusion | flops 379387904 | bytes 3280384 | tf_op jit(solution)/shard_map/dot_general | solution.py:182
  18.6 1.3 all-to-all-done
  20.0 6.7 %all-to-all-start.1 = ((f32[16,32,640]{2,1,0:T(8,128)}), f32[16,32,640]{2,1,0:T(8,128)S(1)}, u32[]{:S(2)}, u32[]{:S(2)}) async-start(f32[16,32,640]{2,1,0:T(8,128)} %bitcast.6), calls=%async_computation.1 | async-start | bytes 2621440 | tf_op jit(solution)/shard_map/all_to_all | solution.py:192
  27.0 1.3 copy.81
  28.3 2.4 %copy.82 = f32[4,2,16,2,16,8]{2,5,4,3,1,0:T(8,128)} copy(f32[4,2,16,2,16,8]{4,3,5,2,1,0:T(2,128)} %bitcast.67) | data formatting | bytes 262144 | tf_op jit(solution)/shard_map/transpose | solution.py:195
  30.7 2.1 %fusion.47 = (f32[4,1,16,2,128]{2,4,3,1,0:T(8,128)}, f32[4,1,16,2,128]{2,4,3,1,0:T(8,128)S(1)}) fusion(f32[4,2,16,2,128]{2,4,3,1,0:T(8,128)} %bitcast.66), kind=kLoop, calls=%fused_computation.91 | loop fusion | bytes 262144 | tf_op jit(solution)/shard_map/slice | solution.py:27
  32.8 1.2 copy.92
  34.9 22.2 %all-to-all-done.1 = f32[16,32,640]{2,1,0:T(8,128)S(1)} async-done(((f32[16,32,640]{2,1,0:T(8,128)}), f32[16,32,640]{2,1,0:T(8,128)S(1)}, u32[]{:S(2)}, u32[]{:S(2)}) %all-to-all-start.1) | async-done | bytes 1310752 | tf_op jit(solution)/shard_map/all_to_all | solution.py:192
  57.1 1.5 %copy.79 = f32[512,640]{0,1:T(8,128)} copy(f32[512,640]{1,0:T(8,128)S(1)} %bitcast.64) | data formatting | bytes 2621440 | tf_op jit(solution)/shard_map/all_to_all | solution.py:192
  58.6 1.5 %fusion.2 = (bf16[640,512]{1,0:T(8,128)(2,1)S(1)}, bf16[640,512]{1,0:T(8,128)(2,1)S(1)}) fusion(f32[512,640]{0,1:T(8,128)} %copy.79), kind=kLoop, calls=%fused_computation.6 | loop fusion | flops 1310720 | bytes 2621440 | tf_op jit(solution)/shard_map/convert_element_type | solution.py:151
  60.2 1.0 shard_map.116
  62.0 1.4 %collective-permute-start.17 = (f32[16,2,16,128]{3,2,1,0:T(8,128)S(1)}, f32[16,2,16,128]{3,2,1,0:T(8,128)S(1)}, u32[]{:S(2)}, u32[]{:S(2)}) collective-permute-start(f32[16,2,16,128]{3,2,1,0:T(8,128)S(1)} %get-tuple-element.197), channel_id=1, source_target_pairs={{1,0},{2,1},{3,2},{4,3},{5,4},{6,5},{7,6},{8,7},{9,8},{10,9},{11,1... | collective-permute-start | bytes 786440 | tf_op jit(solution)/shard_map/ppermute | solution.py:23
  63.9 1.5 %collective-permute-start.1 = (f32[16,2,8,128]{3,2,1,0:T(8,128)S(1)}, f32[16,2,8,128]{3,2,1,0:T(8,128)S(1)}, u32[]{:S(2)}, u32[]{:S(2)}) collective-permute-start(f32[16,2,8,128]{3,2,1,0:T(8,128)S(1)} %get-tuple-element.169), channel_id=1, source_target_pairs={{1,0},{2,1},{3,2},{4,3},{5,4},{6,5},{7,6},{8,7},{9,8},{10,9},{11,1... | collective-permute-start | bytes 393224 | tf_op jit(solution)/shard_map/ppermute | solution.py:23
  65.4 1.0 shard_map.118
  66.4 6.7 %collective-permute-done.refs_1_ = f32[16,2,8,128]{3,2,1,0:T(8,128)S(1)} collective-permute-done((f32[16,2,8,128]{3,2,1,0:T(8,128)S(1)}, f32[16,2,8,128]{3,2,1,0:T(8,128)S(1)}, u32[]{:S(2)}, u32[]{:S(2)}) %collective-permute-start) | collective-permute-done | bytes 131104 | tf_op jit(solution)/shard_map/ppermute | solution.py:23
  73.9 1.8 %collective-permute-start.9 = (f32[16,2,16,128]{3,2,1,0:T(8,128)S(1)}, f32[16,2,16,128]{3,2,1,0:T(8,128)S(1)}, u32[]{:S(2)}, u32[]{:S(2)}) collective-permute-start(f32[16,2,16,128]{3,2,1,0:T(8,128)S(1)} %get-tuple-element.183), channel_id=1, source_target_pairs={{1,0},{2,1},{3,2},{4,3},{5,4},{6,5},{7,6},{8,7},{9,8},{10,9},{11,1... | collective-permute-start | bytes 786440 | tf_op jit(solution)/shard_map/ppermute | solution.py:23
  75.7 0.5 shard_map.129
  76.3 1.7 %collective-permute-start.19 = (f32[16,2,16,128]{3,2,1,0:T(8,128)S(1)}, f32[16,2,16,128]{3,2,1,0:T(8,128)S(1)}, u32[]{:S(2)}, u32[]{:S(2)}) collective-permute-start(f32[16,2,16,128]{3,2,1,0:T(8,128)S(1)} %get-tuple-element.200), channel_id=1, source_target_pairs={{1,0},{2,1},{3,2},{4,3},{5,4},{6,5},{7,6},{8,7},{9,8},{10,9},{11,1... | collective-permute-start | bytes 786440 | tf_op jit(solution)/shard_map/ppermute | solution.py:23
  78.0 1.0 shard_map.120
  79.0 10.8 %collective-permute-done.3.refs_2_ = f32[16,2,8,128]{3,2,1,0:T(8,128)S(1)} collective-permute-done((f32[16,2,8,128]{3,2,1,0:T(8,128)S(1)}, f32[16,2,8,128]{3,2,1,0:T(8,128)S(1)}, u32[]{:S(2)}, u32[]{:S(2)}) %collective-permute-start.3) | collective-permute-done | bytes 131104 | tf_op jit(solution)/shard_map/ppermute | solution.py:23
  90.1 0.5 shard_map.125
  90.7 2.0 %collective-permute-start.11 = (f32[16,2,16,128]{3,2,1,0:T(8,128)S(1)}, f32[16,2,16,128]{3,2,1,0:T(8,128)S(1)}, u32[]{:S(2)}, u32[]{:S(2)}) collective-permute-start(f32[16,2,16,128]{3,2,1,0:T(8,128)S(1)} %get-tuple-element.186), channel_id=1, source_target_pairs={{1,0},{2,1},{3,2},{4,3},{5,4},{6,5},{7,6},{8,7},{9,8},{10,9},{11,1... | collective-permute-start | bytes 786440 | tf_op jit(solution)/shard_map/ppermute | solution.py:23
  92.6 0.5 shard_map.130
  93.1 1.1 collective-permute-start.20
  94.3 0.7 collective-permute-start.21
  94.9 1.4 %collective-permute-start.5 = (f32[16,2,8,128]{3,2,1,0:T(8,128)S(1)}, f32[16,2,8,128]{3,2,1,0:T(8,128)S(1)}, u32[]{:S(2)}, u32[]{:S(2)}) collective-permute-start(f32[16,2,8,128]{3,2,1,0:T(8,128)S(1)} %get-tuple-element.176), channel_id=1, source_target_pairs={{1,0},{2,1},{3,2},{4,3},{5,4},{6,5},{7,6},{8,7},{9,8},{10,9},{11,1... | collective-permute-start | bytes 393224 | tf_op jit(solution)/shard_map/ppermute | solution.py:23
  96.3 0.9 shard_map.122
  97.3 10.5 %collective-permute-done.5.refs_2_ = f32[16,2,8,128]{3,2,1,0:T(8,128)S(1)} collective-permute-done((f32[16,2,8,128]{3,2,1,0:T(8,128)S(1)}, f32[16,2,8,128]{3,2,1,0:T(8,128)S(1)}, u32[]{:S(2)}, u32[]{:S(2)}) %collective-permute-start.5) | collective-permute-done | bytes 131104 | tf_op jit(solution)/shard_map/ppermute | solution.py:23
  108.1 1.9 %collective-permute-start.7 = (f32[16,2,8,128]{3,2,1,0:T(8,128)S(1)}, f32[16,2,8,128]{3,2,1,0:T(8,128)S(1)}, u32[]{:S(2)}, u32[]{:S(2)}) collective-permute-start(f32[16,2,8,128]{3,2,1,0:T(8,128)S(1)} %get-tuple-element.180), channel_id=1, source_target_pairs={{1,0},{2,1},{3,2},{4,3},{5,4},{6,5},{7,6},{8,7},{9,8},{10,9},{11,1... | collective-permute-start | bytes 393224 | tf_op jit(solution)/shard_map/ppermute | solution.py:23
  110.0 0.5 shard_map.126
  110.6 1.7 %collective-permute-start.13 = (f32[16,2,16,128]{3,2,1,0:T(8,128)S(1)}, f32[16,2,16,128]{3,2,1,0:T(8,128)S(1)}, u32[]{:S(2)}, u32[]{:S(2)}) collective-permute-start(f32[16,2,16,128]{3,2,1,0:T(8,128)S(1)} %get-tuple-element.190), channel_id=1, source_target_pairs={{1,0},{2,1},{3,2},{4,3},{5,4},{6,5},{7,6},{8,7},{9,8},{10,9},{11,1... | collective-permute-start | bytes 786440 | tf_op jit(solution)/shard_map/ppermute | solution.py:23
  112.3 0.5 shard_map.131
  112.9 1.7 %collective-permute-start.23 = (f32[16,2,16,128]{3,2,1,0:T(8,128)S(1)}, f32[16,2,16,128]{3,2,1,0:T(8,128)S(1)}, u32[]{:S(2)}, u32[]{:S(2)}) collective-permute-start(f32[16,2,16,128]{3,2,1,0:T(8,128)S(1)} %get-tuple-element.208), channel_id=1, source_target_pairs={{1,0},{2,1},{3,2},{4,3},{5,4},{6,5},{7,6},{8,7},{9,8},{10,9},{11,1... | collective-permute-start | bytes 786440 | tf_op jit(solution)/shard_map/ppermute | solution.py:23
  114.7 7.8 %collective-permute-done.12.refs_1_ = f32[16,2,16,128]{3,2,1,0:T(8,128)S(1)} collective-permute-done((f32[16,2,16,128]{3,2,1,0:T(8,128)S(1)}, f32[16,2,16,128]{3,2,1,0:T(8,128)S(1)}, u32[]{:S(2)}, u32[]{:S(2)}) %collective-permute-start.12) | collective-permute-done | bytes 262176 | tf_op jit(solution)/shard_map/ppermute | solution.py:23
  122.4 1.3 collective-permute-done.13.refs_2_
  124.3 2.0 %collective-permute-start.15 = (f32[16,2,16,128]{3,2,1,0:T(8,128)S(1)}, f32[16,2,16,128]{3,2,1,0:T(8,128)S(1)}, u32[]{:S(2)}, u32[]{:S(2)}) collective-permute-start(f32[16,2,16,128]{3,2,1,0:T(8,128)S(1)} %get-tuple-element.194), channel_id=1, source_target_pairs={{1,0},{2,1},{3,2},{4,3},{5,4},{6,5},{7,6},{8,7},{9,8},{10,9},{11,1... | collective-permute-start | bytes 786440 | tf_op jit(solution)/shard_map/ppermute | solution.py:23
  126.6 6.4 %collective-permute-done.14 = f32[16,2,16,128]{3,2,1,0:T(8,128)S(1)} collective-permute-done((f32[16,2,16,128]{3,2,1,0:T(8,128)S(1)}, f32[16,2,16,128]{3,2,1,0:T(8,128)S(1)}, u32[]{:S(2)}, u32[]{:S(2)}) %collective-permute-start.14) | collective-permute-done | bytes 262176 | tf_op jit(solution)/shard_map/ppermute | solution.py:23
  133.2 1.2 copy.88
  134.4 0.6 copy.89
  (82 shorter events, 6.3 us)
Async XLA Ops:
  7.2 7.9 %copy-start.2 = (f32[256,640]{1,0:T(8,128)S(1)}, f32[256,640]{1,0:T(8,128)}, u32[]{:S(2)}) copy-start(f32[256,640]{1,0:T(8,128)} %param.34) | copy-start | bytes 1966084
  8.8 11.2 %all-to-all-start = ((f32[16,1,2080]{2,1,0:T(1,128)}), f32[16,1,2080]{2,1,0:T(1,128)S(1)}, u32[]{:S(2)}, u32[]{:S(2)}) async-start(f32[16,1,2080]{2,1,0:T(1,128)} %all_to_all.16), calls=%async_computation | async-start | bytes 278528 | tf_op jit(solution)/shard_map/all_to_all | solution.py:191
  15.9 2.2 %copy-start.1 = (f32[40,16,2,128]{3,2,1,0:T(2,128)S(1)}, f32[40,16,2,128]{3,2,1,0:T(2,128)}, u32[]{:S(2)}) copy-start(f32[40,16,2,128]{3,2,1,0:T(2,128)} %param.31) | copy-start | bytes 1966084
  20.0 37.2 %all-to-all-start.1 = ((f32[16,32,640]{2,1,0:T(8,128)}), f32[16,32,640]{2,1,0:T(8,128)S(1)}, u32[]{:S(2)}, u32[]{:S(2)}) async-start(f32[16,32,640]{2,1,0:T(8,128)} %bitcast.6), calls=%async_computation.1 | async-start | bytes 2621440 | tf_op jit(solution)/shard_map/all_to_all | solution.py:192
  60.2 1.0 copy-start
  61.6 14.1 %collective-permute-start.16 = (f32[16,2,16,128]{3,2,1,0:T(8,128)S(1)}, f32[16,2,16,128]{3,2,1,0:T(8,128)S(1)}, u32[]{:S(2)}, u32[]{:S(2)}) collective-permute-start(f32[16,2,16,128]{3,2,1,0:T(8,128)S(1)} %get-tuple-element.196), channel_id=1, source_target_pairs={{15,0},{0,1},{1,2},{2,3},{3,4},{4,5},{5,6},{6,7},{7,8},{8,9},{9,10... | collective-permute-start | bytes 786440 | tf_op jit(solution)/shard_map/ppermute | solution.py:23
  62.0 13.8 %collective-permute-start.17 = (f32[16,2,16,128]{3,2,1,0:T(8,128)S(1)}, f32[16,2,16,128]{3,2,1,0:T(8,128)S(1)}, u32[]{:S(2)}, u32[]{:S(2)}) collective-permute-start(f32[16,2,16,128]{3,2,1,0:T(8,128)S(1)} %get-tuple-element.197), channel_id=1, source_target_pairs={{1,0},{2,1},{3,2},{4,3},{5,4},{6,5},{7,6},{8,7},{9,8},{10,9},{11,1... | collective-permute-start | bytes 786440 | tf_op jit(solution)/shard_map/ppermute | solution.py:23
  63.6 9.4 %collective-permute-start = (f32[16,2,8,128]{3,2,1,0:T(8,128)S(1)}, f32[16,2,8,128]{3,2,1,0:T(8,128)S(1)}, u32[]{:S(2)}, u32[]{:S(2)}) collective-permute-start(f32[16,2,8,128]{3,2,1,0:T(8,128)S(1)} %get-tuple-element.168), channel_id=1, source_target_pairs={{15,0},{0,1},{1,2},{2,3},{3,4},{4,5},{5,6},{6,7},{7,8},{8,9},{9,10... | collective-permute-start | bytes 393224 | tf_op jit(solution)/shard_map/ppermute | solution.py:23
  63.9 9.2 %collective-permute-start.1 = (f32[16,2,8,128]{3,2,1,0:T(8,128)S(1)}, f32[16,2,8,128]{3,2,1,0:T(8,128)S(1)}, u32[]{:S(2)}, u32[]{:S(2)}) collective-permute-start(f32[16,2,8,128]{3,2,1,0:T(8,128)S(1)} %get-tuple-element.169), channel_id=1, source_target_pairs={{1,0},{2,1},{3,2},{4,3},{5,4},{6,5},{7,6},{8,7},{9,8},{10,9},{11,1... | collective-permute-start | bytes 393224 | tf_op jit(solution)/shard_map/ppermute | solution.py:23
  73.3 4.7 %collective-permute-start.2 = (f32[16,2,8,128]{3,2,1,0:T(8,128)S(1)}, f32[16,2,8,128]{3,2,1,0:T(8,128)S(1)}, u32[]{:S(2)}, u32[]{:S(2)}) collective-permute-start(f32[16,2,8,128]{3,2,1,0:T(8,128)S(1)} %get-tuple-element.171), channel_id=1, source_target_pairs={{15,0},{0,1},{1,2},{2,3},{3,4},{4,5},{5,6},{6,7},{7,8},{8,9},{9,10... | collective-permute-start | bytes 393224 | tf_op jit(solution)/shard_map/ppermute | solution.py:23
  73.9 16.2 %collective-permute-start.8 = (f32[16,2,16,128]{3,2,1,0:T(8,128)S(1)}, f32[16,2,16,128]{3,2,1,0:T(8,128)S(1)}, u32[]{:S(2)}, u32[]{:S(2)}) collective-permute-start(f32[16,2,16,128]{3,2,1,0:T(8,128)S(1)} %get-tuple-element.182), channel_id=1, source_target_pairs={{15,0},{0,1},{1,2},{2,3},{3,4},{4,5},{5,6},{6,7},{7,8},{8,9},{9,10... | collective-permute-start | bytes 786440 | tf_op jit(solution)/shard_map/ppermute | solution.py:23
  73.9 16.2 %collective-permute-start.9 = (f32[16,2,16,128]{3,2,1,0:T(8,128)S(1)}, f32[16,2,16,128]{3,2,1,0:T(8,128)S(1)}, u32[]{:S(2)}, u32[]{:S(2)}) collective-permute-start(f32[16,2,16,128]{3,2,1,0:T(8,128)S(1)} %get-tuple-element.183), channel_id=1, source_target_pairs={{1,0},{2,1},{3,2},{4,3},{5,4},{6,5},{7,6},{8,7},{9,8},{10,9},{11,1... | collective-permute-start | bytes 786440 | tf_op jit(solution)/shard_map/ppermute | solution.py:23
  76.2 16.4 %collective-permute-start.18 = (f32[16,2,16,128]{3,2,1,0:T(8,128)S(1)}, f32[16,2,16,128]{3,2,1,0:T(8,128)S(1)}, u32[]{:S(2)}, u32[]{:S(2)}) collective-permute-start(f32[16,2,16,128]{3,2,1,0:T(8,128)S(1)} %get-tuple-element.199), channel_id=1, source_target_pairs={{15,0},{0,1},{1,2},{2,3},{3,4},{4,5},{5,6},{6,7},{7,8},{8,9},{9,10... | collective-permute-start | bytes 786440 | tf_op jit(solution)/shard_map/ppermute | solution.py:23
  76.3 16.4 %collective-permute-start.19 = (f32[16,2,16,128]{3,2,1,0:T(8,128)S(1)}, f32[16,2,16,128]{3,2,1,0:T(8,128)S(1)}, u32[]{:S(2)}, u32[]{:S(2)}) collective-permute-start(f32[16,2,16,128]{3,2,1,0:T(8,128)S(1)} %get-tuple-element.200), channel_id=1, source_target_pairs={{1,0},{2,1},{3,2},{4,3},{5,4},{6,5},{7,6},{8,7},{9,8},{10,9},{11,1... | collective-permute-start | bytes 786440 | tf_op jit(solution)/shard_map/ppermute | solution.py:23
  78.0 11.8 %collective-permute-start.3 = (f32[16,2,8,128]{3,2,1,0:T(8,128)S(1)}, f32[16,2,8,128]{3,2,1,0:T(8,128)S(1)}, u32[]{:S(2)}, u32[]{:S(2)}) collective-permute-start(f32[16,2,8,128]{3,2,1,0:T(8,128)S(1)} %get-tuple-element.172), channel_id=1, source_target_pairs={{1,0},{2,1},{3,2},{4,3},{5,4},{6,5},{7,6},{8,7},{9,8},{10,9},{11,1... | collective-permute-start | bytes 393224 | tf_op jit(solution)/shard_map/ppermute | solution.py:23
  90.0 4.9 %collective-permute-start.4 = (f32[16,2,8,128]{3,2,1,0:T(8,128)S(1)}, f32[16,2,8,128]{3,2,1,0:T(8,128)S(1)}, u32[]{:S(2)}, u32[]{:S(2)}) collective-permute-start(f32[16,2,8,128]{3,2,1,0:T(8,128)S(1)} %get-tuple-element.175), channel_id=1, source_target_pairs={{15,0},{0,1},{1,2},{2,3},{3,4},{4,5},{5,6},{6,7},{7,8},{8,9},{9,10... | collective-permute-start | bytes 393224 | tf_op jit(solution)/shard_map/ppermute | solution.py:23
  90.6 17.5 %collective-permute-start.10 = (f32[16,2,16,128]{3,2,1,0:T(8,128)S(1)}, f32[16,2,16,128]{3,2,1,0:T(8,128)S(1)}, u32[]{:S(2)}, u32[]{:S(2)}) collective-permute-start(f32[16,2,16,128]{3,2,1,0:T(8,128)S(1)} %get-tuple-element.185), channel_id=1, source_target_pairs={{15,0},{0,1},{1,2},{2,3},{3,4},{4,5},{5,6},{6,7},{7,8},{8,9},{9,10... | collective-permute-start | bytes 786440 | tf_op jit(solution)/shard_map/ppermute | solution.py:23
  90.7 19.4 %collective-permute-start.11 = (f32[16,2,16,128]{3,2,1,0:T(8,128)S(1)}, f32[16,2,16,128]{3,2,1,0:T(8,128)S(1)}, u32[]{:S(2)}, u32[]{:S(2)}) collective-permute-start(f32[16,2,16,128]{3,2,1,0:T(8,128)S(1)} %get-tuple-element.186), channel_id=1, source_target_pairs={{1,0},{2,1},{3,2},{4,3},{5,4},{6,5},{7,6},{8,7},{9,8},{10,9},{11,1... | collective-permute-start | bytes 786440 | tf_op jit(solution)/shard_map/ppermute | solution.py:23
  93.1 17.5 %collective-permute-start.20 = (f32[16,2,16,128]{3,2,1,0:T(8,128)S(1)}, f32[16,2,16,128]{3,2,1,0:T(8,128)S(1)}, u32[]{:S(2)}, u32[]{:S(2)}) collective-permute-start(f32[16,2,16,128]{3,2,1,0:T(8,128)S(1)} %get-tuple-element.203), channel_id=1, source_target_pairs={{15,0},{0,1},{1,2},{2,3},{3,4},{4,5},{5,6},{6,7},{7,8},{8,9},{9,10... | collective-permute-start | bytes 786440 | tf_op jit(solution)/shard_map/ppermute | solution.py:23
  94.3 18.1 %collective-permute-start.21 = (f32[16,2,16,128]{3,2,1,0:T(8,128)S(1)}, f32[16,2,16,128]{3,2,1,0:T(8,128)S(1)}, u32[]{:S(2)}, u32[]{:S(2)}) collective-permute-start(f32[16,2,16,128]{3,2,1,0:T(8,128)S(1)} %get-tuple-element.204), channel_id=1, source_target_pairs={{1,0},{2,1},{3,2},{4,3},{5,4},{6,5},{7,6},{8,7},{9,8},{10,9},{11,1... | collective-permute-start | bytes 786440 | tf_op jit(solution)/shard_map/ppermute | solution.py:23
  94.9 12.8 %collective-permute-start.5 = (f32[16,2,8,128]{3,2,1,0:T(8,128)S(1)}, f32[16,2,8,128]{3,2,1,0:T(8,128)S(1)}, u32[]{:S(2)}, u32[]{:S(2)}) collective-permute-start(f32[16,2,8,128]{3,2,1,0:T(8,128)S(1)} %get-tuple-element.176), channel_id=1, source_target_pairs={{1,0},{2,1},{3,2},{4,3},{5,4},{6,5},{7,6},{8,7},{9,8},{10,9},{11,1... | collective-permute-start | bytes 393224 | tf_op jit(solution)/shard_map/ppermute | solution.py:23
  108.0 4.9 %collective-permute-start.6 = (f32[16,2,8,128]{3,2,1,0:T(8,128)S(1)}, f32[16,2,8,128]{3,2,1,0:T(8,128)S(1)}, u32[]{:S(2)}, u32[]{:S(2)}) collective-permute-start(f32[16,2,8,128]{3,2,1,0:T(8,128)S(1)} %get-tuple-element.179), channel_id=1, source_target_pairs={{15,0},{0,1},{1,2},{2,3},{3,4},{4,5},{5,6},{6,7},{7,8},{8,9},{9,10... | collective-permute-start | bytes 393224 | tf_op jit(solution)/shard_map/ppermute | solution.py:23
  108.1 6.5 %collective-permute-start.7 = (f32[16,2,8,128]{3,2,1,0:T(8,128)S(1)}, f32[16,2,8,128]{3,2,1,0:T(8,128)S(1)}, u32[]{:S(2)}, u32[]{:S(2)}) collective-permute-start(f32[16,2,8,128]{3,2,1,0:T(8,128)S(1)} %get-tuple-element.180), channel_id=1, source_target_pairs={{1,0},{2,1},{3,2},{4,3},{5,4},{6,5},{7,6},{8,7},{9,8},{10,9},{11,1... | collective-permute-start | bytes 393224 | tf_op jit(solution)/shard_map/ppermute | solution.py:23
  110.5 11.9 %collective-permute-start.12 = (f32[16,2,16,128]{3,2,1,0:T(8,128)S(1)}, f32[16,2,16,128]{3,2,1,0:T(8,128)S(1)}, u32[]{:S(2)}, u32[]{:S(2)}) collective-permute-start(f32[16,2,16,128]{3,2,1,0:T(8,128)S(1)} %get-tuple-element.189), channel_id=1, source_target_pairs={{15,0},{0,1},{1,2},{2,3},{3,4},{4,5},{5,6},{6,7},{7,8},{8,9},{9,10... | collective-permute-start | bytes 786440 | tf_op jit(solution)/shard_map/ppermute | solution.py:23
  110.6 13.1 %collective-permute-start.13 = (f32[16,2,16,128]{3,2,1,0:T(8,128)S(1)}, f32[16,2,16,128]{3,2,1,0:T(8,128)S(1)}, u32[]{:S(2)}, u32[]{:S(2)}) collective-permute-start(f32[16,2,16,128]{3,2,1,0:T(8,128)S(1)} %get-tuple-element.190), channel_id=1, source_target_pairs={{1,0},{2,1},{3,2},{4,3},{5,4},{6,5},{7,6},{8,7},{9,8},{10,9},{11,1... | collective-permute-start | bytes 786440 | tf_op jit(solution)/shard_map/ppermute | solution.py:23
  112.8 13.4 %collective-permute-start.22 = (f32[16,2,16,128]{3,2,1,0:T(8,128)S(1)}, f32[16,2,16,128]{3,2,1,0:T(8,128)S(1)}, u32[]{:S(2)}, u32[]{:S(2)}) collective-permute-start(f32[16,2,16,128]{3,2,1,0:T(8,128)S(1)} %get-tuple-element.207), channel_id=1, source_target_pairs={{15,0},{0,1},{1,2},{2,3},{3,4},{4,5},{5,6},{6,7},{7,8},{8,9},{9,10... | collective-permute-start | bytes 786440 | tf_op jit(solution)/shard_map/ppermute | solution.py:23
  112.9 13.6 %collective-permute-start.23 = (f32[16,2,16,128]{3,2,1,0:T(8,128)S(1)}, f32[16,2,16,128]{3,2,1,0:T(8,128)S(1)}, u32[]{:S(2)}, u32[]{:S(2)}) collective-permute-start(f32[16,2,16,128]{3,2,1,0:T(8,128)S(1)} %get-tuple-element.208), channel_id=1, source_target_pairs={{1,0},{2,1},{3,2},{4,3},{5,4},{6,5},{7,6},{8,7},{9,8},{10,9},{11,1... | collective-permute-start | bytes 786440 | tf_op jit(solution)/shard_map/ppermute | solution.py:23
  124.2 8.8 %collective-permute-start.14 = (f32[16,2,16,128]{3,2,1,0:T(8,128)S(1)}, f32[16,2,16,128]{3,2,1,0:T(8,128)S(1)}, u32[]{:S(2)}, u32[]{:S(2)}) collective-permute-start(f32[16,2,16,128]{3,2,1,0:T(8,128)S(1)} %get-tuple-element.193), channel_id=1, source_target_pairs={{15,0},{0,1},{1,2},{2,3},{3,4},{4,5},{5,6},{6,7},{7,8},{8,9},{9,10... | collective-permute-start | bytes 786440 | tf_op jit(solution)/shard_map/ppermute | solution.py:23
  124.3 8.8 %collective-permute-start.15 = (f32[16,2,16,128]{3,2,1,0:T(8,128)S(1)}, f32[16,2,16,128]{3,2,1,0:T(8,128)S(1)}, u32[]{:S(2)}, u32[]{:S(2)}) collective-permute-start(f32[16,2,16,128]{3,2,1,0:T(8,128)S(1)} %get-tuple-element.194), channel_id=1, source_target_pairs={{1,0},{2,1},{3,2},{4,3},{5,4},{6,5},{7,6},{8,7},{9,8},{10,9},{11,1... | collective-permute-start | bytes 786440 | tf_op jit(solution)/shard_map/ppermute | solution.py:23
